TPU v7x, 512 devices: a whole 4x8x8 slice. The times are simulated.
512 devices in a mesh: width: 16 (over z, core), hidden: 32 (over y, x).
Axes of the slice: x: 4, y: 8, z: 8, core: 2. Of those that a mesh axis runs over, the one named last changes fastest.
Arguments:
- tokens: bfloat16 [2, 512, 18432], P(None, 'hidden', 'width'), may hold values from -1000 to 1000
- gain: float32 [18432], P('width'), may hold values from 0.5 to 2
- query_weight: bfloat16 [18432, 12288], P('width', 'hidden'), may hold values from -0.063570226 to 0.063570226
- keyval_weight: bfloat16 [18432, 512], P('width', 'hidden'), may hold values from -0.046875 to 0.046875
- out_weight: bfloat16 [12288, 18432], P('hidden', 'width'), may hold values from -0.0546875 to 0.0546875
- key_cache: bfloat16 [512, 2048, 256], P(('hidden', 'width')), may hold values from -8 to 8
- value_cache: bfloat16 [512, 2048, 256], P(('hidden', 'width')), may hold values from -6 to 6
- lengths: int32 [512], P(('hidden', 'width')), may hold values from 2 to 2048, as said below
Outputs:
- attn_out: bfloat16 [2, 512, 18432], P(None, 'hidden', 'width')
Inputs may be any that keep to these rules, and one draw needn't show every extreme that they name: `lengths`: every row attends to at least two cached positions; some row attends to all 2048.
All inputs are finite; a program needn't handle non-finite values.
Results may differ from a plain program's by a relative error of at most 0.04.
Values may be sent and summed in bfloat16 or wider, within the bound.
A program may use at most 64 MiB of HBM per device.

v0:
```python
import jax
import jax.numpy as jnp
from jax import lax
from jax.sharding import PartitionSpec as P

D = 18432
HEADS = 48
HEAD_DIM = 256


EPS = 1e-05
MASKED_SCORE = -1e30


def normalize(token_rows, gain):
    values = token_rows.astype(jnp.float32)
    average = lax.psum(jnp.sum(values, axis=1), "width") / D
    centered = values - average[:, None]
    spread = lax.psum(jnp.sum(centered * centered, axis=1), "width") / D
    return (centered * lax.rsqrt(spread + EPS)[:, None] * gain[None, :]).astype(jnp.bfloat16)


def to_attention_rows(query_part, keyval_part):
    moved_query, moved_keyval = (
        lax.all_to_all(
            query_part.astype(jnp.bfloat16), "hidden", split_axis=0, concat_axis=1, tiled=True
        ).astype(query_part.dtype),
        lax.all_to_all(
            keyval_part.astype(jnp.bfloat16), "hidden", split_axis=0, concat_axis=1, tiled=True
        ).astype(keyval_part.dtype),
    )
    return (
        lax.psum_scatter(
            moved_query.astype(jnp.bfloat16), "width", scatter_dimension=0, tiled=True
        ).astype(jnp.float32),
        lax.psum_scatter(
            moved_keyval.astype(jnp.bfloat16), "width", scatter_dimension=0, tiled=True
        ).astype(jnp.float32),
    )


def to_feature_rows(attended):
    gathered = lax.all_gather(attended, "width", axis=0, tiled=True)
    return lax.all_to_all(gathered, "hidden", split_axis=1, concat_axis=0, tiled=True)


def attend(queries, key_cache, value_cache, usable, stacked_keys, stacked_values):
    inv_root = HEAD_DIM ** (-0.5)
    cached_scores = (
        jnp.einsum("rhd,rkd->rhk", queries, key_cache, preferred_element_type=jnp.float32)
        * inv_root
    )
    cached_scores = jnp.where(usable[:, None, :], cached_scores, MASKED_SCORE)
    fresh_scores = (
        jnp.einsum("rhd,rkd->rhk", queries, stacked_keys, preferred_element_type=jnp.float32)
        * inv_root
    )
    row_peak = jnp.maximum(jnp.max(cached_scores, axis=2), jnp.max(fresh_scores, axis=2))
    cached_weights = jnp.where(
        usable[:, None, :], jnp.exp(cached_scores - row_peak[:, :, None]), 0.0
    )
    fresh_weights = jnp.exp(fresh_scores - row_peak[:, :, None])
    weight_total = jnp.sum(cached_weights, axis=2) + jnp.sum(fresh_weights, axis=2)
    weighted = jnp.einsum(
        "rhk,rkd->rhd",
        cached_weights.astype(jnp.bfloat16),
        value_cache,
        preferred_element_type=jnp.float32,
    )
    weighted = weighted + jnp.einsum(
        "rhk,rkd->rhd",
        fresh_weights.astype(jnp.bfloat16),
        stacked_values,
        preferred_element_type=jnp.float32,
    )
    return (weighted / weight_total[:, :, None]).astype(jnp.bfloat16)


def shards(tokens, gain, query_weight, keyval_weight, out_weight, key_cache, value_cache, lengths):
    feat_dev = query_weight.shape[1]
    att_rows = key_cache.shape[0]
    cache_len = key_cache.shape[1]
    joint_weight = jnp.concatenate([query_weight, keyval_weight], axis=1)
    positions = jnp.arange(cache_len, dtype=jnp.int32)
    usable = positions[None, :] < lengths[:, None]
    keys_new = []
    values_new = []
    results = []
    for decode_step in range(tokens.shape[0]):
        normed = normalize(tokens[decode_step], gain)
        projected = jnp.dot(
            lax.all_gather(normed, "hidden", axis=0, tiled=True),
            joint_weight,
            preferred_element_type=jnp.float32,
        )
        summed_query, summed_keyval = to_attention_rows(
            projected[:, :feat_dev], projected[:, feat_dev:]
        )
        queries = summed_query.astype(jnp.bfloat16).reshape(att_rows, HEADS, HEAD_DIM)
        keyval = summed_keyval.astype(jnp.bfloat16)
        keys_new.append(keyval[:, :HEAD_DIM])
        values_new.append(keyval[:, HEAD_DIM:])
        stacked_keys = jnp.stack(keys_new, axis=1)
        stacked_values = jnp.stack(values_new, axis=1)
        attended = attend(queries, key_cache, value_cache, usable, stacked_keys, stacked_values)
        feature_rows = to_feature_rows(attended.reshape(att_rows, HEADS * HEAD_DIM))
        summed_out = lax.psum_scatter(
            jnp.dot(feature_rows, out_weight, preferred_element_type=jnp.float32).astype(
                jnp.bfloat16
            ),
            "hidden",
            scatter_dimension=0,
            tiled=True,
        )
        results.append(summed_out)
    return jnp.stack(results, axis=0)


def solution(mesh):
    return jax.shard_map(
        shards,
        mesh=mesh,
        in_specs=(
            P(None, "hidden", "width"),
            P("width"),
            P("width", "hidden"),
            P("width", "hidden"),
            P("hidden", "width"),
            P(("hidden", "width"), None, None),
            P(("hidden", "width"), None, None),
            P(("hidden", "width")),
        ),
        out_specs=P(None, "hidden", "width"),
        check_vma=False,
    )
```

profile of v0, /device:TPU:1, one launch (start us, length us, event | category | flops | bytes accessed | tf_op | source)
XLA Modules:
  0.0 838.4 jit_solution(13148507402919033438)
XLA Ops:
  6.5 1.0 convert_reduce_fusion.1
  7.5 30.6 %all-reduce.5 = (f32[16]{0:T(128)S(1)}, f32[16]{0:T(128)S(1)}) all-reduce(f32[16]{0:T(128)S(1)} %get-tuple-element.7, f32[16]{0:T(128)S(1)} %get-tuple-element.8), channel_id=1, replica_groups=mesh['width'=16,'hidden'=32] {'width'}, use_global_device_ids=true, to_apply=%region_1.0 | all-reduce | flops 32 | bytes 256 | tf_op jit(solution)/shard_map/psum | solution.py:17
  39.1 25.8 %all-reduce.4 = (f32[16]{0:T(128)S(1)}, f32[16]{0:T(128)S(1)}) all-reduce(f32[16]{0:T(128)S(1)} %get-tuple-element.6, f32[16]{0:T(128)S(1)} %get-tuple-element.5), channel_id=1, replica_groups=mesh['width'=16,'hidden'=32] {'width'}, use_global_device_ids=true, to_apply=%region_12.13 | all-reduce | flops 32 | bytes 256 | tf_op jit(solution)/shard_map/psum | solution.py:19
  64.9 1.5 fusion.29
  68.2 72.0 %all-gather.5.cloned.1.call-done = bf16[512,1152]{1,0:T(8,128)(2,1)} async-done(((bf16[16,1152]{1,0:T(8,128)(2,1)}), bf16[512,1152]{1,0:T(8,128)(2,1)}) %all-gather.5.cloned.1.call-update) | async-done | bytes 1179664 | tf_op jit(solution)/shard_map/all_gather | solution.py:92
  140.2 2.3 convolution_convert_fusion.3
  143.5 5.7 all-to-all-start
  149.2 74.0 %all-gather.7.cloned.1.call-done = bf16[512,1152]{1,0:T(8,128)(2,1)} async-done(((bf16[16,1152]{1,0:T(8,128)(2,1)}), bf16[512,1152]{1,0:T(8,128)(2,1)}) %all-gather.7.cloned.1.call-update) | async-done | bytes 1179664 | tf_op jit(solution)/shard_map/all_gather | solution.py:92
  223.2 2.0 convolution_convert_fusion.2
  226.1 5.7 all-to-all-start.3
  232.6 10.6 %all-to-all-done.3 = bf16[32,16,384]{2,1,0:T(8,128)(2,1)S(1)} async-done(((bf16[32,16,384]{2,1,0:T(8,128)(2,1)}), bf16[32,16,384]{2,1,0:T(8,128)(2,1)S(1)}, u32[]{:S(2)}, u32[]{:S(2)}) %all-to-all-start.3) | async-done | bytes 393248 | tf_op jit(solution)/shard_map/all_to_all | solution.py:25
  245.1 3.9 all-to-all-start.1
  250.6 7.0 all-to-all-done.1
  257.6 3.8 all-to-all-start.4
  261.5 1.3 dynamic-slice
  263.0 6.9 all-to-all-done.4
  270.2 52.4 %all-reduce.6 = (bf16[16,512]{1,0:T(8,128)(2,1)S(1)}, bf16[16,512]{1,0:T(8,128)(2,1)S(1)}) all-reduce(bf16[16,512]{1,0:T(8,128)(2,1)S(1)} %copy.33, bf16[16,512]{1,0:T(8,128)(2,1)S(1)} %copy.32), channel_id=6, replica_groups=mesh['width'=16,'hidden'=32] {'width'}, use_global_device_ids=true, to_apply=%region_15.16.clone | all-reduce | flops 16384 | bytes 65536
  324.0 39.5 %all-reduce.10.cloned.1.call-done = (bf16[16,12288]{1,0:T(8,128)(2,1)}, bf16[16,12288]{1,0:T(8,128)(2,1)}) async-done(((bf16[16,12288]{1,0:T(8,128)(2,1)}, bf16[16,12288]{1,0:T(8,128)(2,1)}), (bf16[16,12288]{1,0:T(8,128)(2,1)}, bf16[16,12288]{1,0:T(8,128)(2,1)})) %all-reduce.10.cloned.1.call-update) | async-done | bytes 786448
  363.5 1.7 dynamic-slice_reduce_fusion.1
  366.5 1.7 dynamic-slice_reduce_fusion
  369.8 19.3 %all-gather = bf16[16,1,12288]{2,1,0:T(2,128)(2,1)} all-gather(bf16[1,1,12288]{2,1,0:T(2,128)(2,1)S(1)} %reshape.194), channel_id=1, replica_groups=mesh['width'=16,'hidden'=32] {'width'}, dimensions={0}, use_global_device_ids=true | all-gather | bytes 417792 | tf_op jit(solution)/shard_map/all_gather | solution.py:43
  389.1 4.2 reduce.15
  393.3 1.0 copy.43
  394.4 23.5 %all_to_all.114 = bf16[16,32,384]{2,0,1:T(8,128)(2,1)S(1)} all-to-all(bf16[16,32,384]{2,0,1:T(8,128)(2,1)S(1)} %bitcast.127), channel_id=1, replica_groups=mesh['width'=16,'hidden'=32] {'hidden'}, dimensions={1} | all-to-all | bytes 786432 | tf_op jit(solution)/shard_map/all_to_all | solution.py:44
  417.9 1.8 convolution_convert_fusion.1
  420.4 20.0 %all-gather.1 = bf16[16,1,12288]{2,1,0:T(2,128)(2,1)S(1)} all-gather(bf16[1,1,12288]{2,1,0:T(2,128)(2,1)S(1)} %reshape.196), channel_id=1, replica_groups=mesh['width'=16,'hidden'=32] {'width'}, dimensions={0}, use_global_device_ids=true | all-gather | bytes 417792 | tf_op jit(solution)/shard_map/all_gather | solution.py:43
  440.4 2.3 reduce.17
  442.7 18.7 %all_to_all.115 = bf16[16,32,384]{2,0,1:T(8,128)(2,1)S(1)} all-to-all(bf16[16,32,384]{2,0,1:T(8,128)(2,1)S(1)} %bitcast.129), channel_id=1, replica_groups=mesh['width'=16,'hidden'=32] {'hidden'}, dimensions={1} | all-to-all | bytes 786432 | tf_op jit(solution)/shard_map/all_to_all | solution.py:44
  461.5 1.9 convolution_convert_fusion
  463.3 155.8 %reduce-scatter.3.cloned.1.call-done = bf16[16,1152]{1,0:T(8,128)(2,1)} async-done(((bf16[512,1152]{1,0:T(8,128)(2,1)}), bf16[16,1152]{1,0:T(8,128)(2,1)}) %reduce-scatter.3.cloned.1.call-update) | async-done | bytes 36880 | tf_op jit(solution)/shard_map/reduce_scatter | solution.py:107
  619.2 211.3 %reduce-scatter.5.cloned.1.call-done = bf16[16,1152]{1,0:T(8,128)(2,1)} async-done(((bf16[512,1152]{1,0:T(8,128)(2,1)}), bf16[16,1152]{1,0:T(8,128)(2,1)}) %reduce-scatter.5.cloned.1.call-update) | async-done | bytes 36880 | tf_op jit(solution)/shard_map/reduce_scatter | solution.py:107
  830.5 1.4 pad_maximum_fusion.3
  (62 shorter events, 13.6 us)
Async XLA Ops:
  6.5 358.7 %copy-start = (bf16[1,2048,256]{2,1,0:T(8,128)(2,1)S(1)}, bf16[1,2048,256]{2,1,0:T(8,128)(2,1)}, u32[]{:S(2)}) copy-start(bf16[1,2048,256]{2,1,0:T(8,128)(2,1)} %param.13) | copy-start | bytes 3145732
  6.5 133.7 %all-gather.5.cloned.1.call-start = ((), (), s32[]{:S(2)}) async-start(), calls=%async_computation.8 | async-start | bytes 1216512 | tf_op jit(solution)/shard_map/all_gather | solution.py:92
  66.5 156.7 %all-gather.7.cloned.1.call-start = ((), (), s32[]{:S(2)}) async-start(), calls=%async_computation.10 | async-start | bytes 1216512 | tf_op jit(solution)/shard_map/all_gather | solution.py:92
  142.5 80.6 %copy-start.3 = (bf16[1152,384]{1,0:T(8,128)(2,1)S(1)}, bf16[1152,384]{1,0:T(8,128)(2,1)}, u32[]{:S(2)}) copy-start(bf16[1152,384]{1,0:T(8,128)(2,1)} %param.10) | copy-start | bytes 2654212
  143.5 82.6 %all-to-all-start = ((bf16[32,16,384]{2,1,0:T(8,128)(2,1)}), bf16[32,16,384]{2,1,0:T(8,128)(2,1)S(1)}, u32[]{:S(2)}, u32[]{:S(2)}) async-start(bf16[32,16,384]{2,1,0:T(8,128)(2,1)} %bitcast.2), calls=%async_computation | async-start | bytes 786432 | tf_op jit(solution)/shard_map/all_to_all | solution.py:25
  226.1 17.1 %all-to-all-start.3 = ((bf16[32,16,384]{2,1,0:T(8,128)(2,1)}), bf16[32,16,384]{2,1,0:T(8,128)(2,1)S(1)}, u32[]{:S(2)}, u32[]{:S(2)}) async-start(bf16[32,16,384]{2,1,0:T(8,128)(2,1)} %bitcast.14), calls=%async_computation.4 | async-start | bytes 786432 | tf_op jit(solution)/shard_map/all_to_all | solution.py:25
  231.8 131.7 %all-reduce.10.cloned.1.call-start = ((), (), s32[]{:S(2)}) async-start(), calls=%async_computation.12 | async-start | bytes 1572864
  245.1 12.5 %all-to-all-start.1 = ((bf16[32,2,128]{2,1,0:T(2,128)(2,1)}), bf16[32,2,128]{2,1,0:T(2,128)(2,1)S(1)}, u32[]{:S(2)}, u32[]{:S(2)}) async-start(bf16[32,2,128]{2,1,0:T(2,128)(2,1)} %reshape.215), calls=%async_computation.1 | async-start | bytes 32768 | tf_op jit(solution)/shard_map/all_to_all | solution.py:28
  257.6 12.4 %all-to-all-start.4 = ((bf16[32,2,128]{2,1,0:T(2,128)(2,1)}), bf16[32,2,128]{2,1,0:T(2,128)(2,1)S(1)}, u32[]{:S(2)}, u32[]{:S(2)}) async-start(bf16[32,2,128]{2,1,0:T(2,128)(2,1)} %reshape.213), calls=%async_computation.5 | async-start | bytes 32768 | tf_op jit(solution)/shard_map/all_to_all | solution.py:28
  261.4 357.7 %reduce-scatter.3.cloned.1.call-start = ((), (), s32[]{:S(2)}) async-start(), calls=%async_computation.9 | async-start | bytes 1216512 | tf_op jit(solution)/shard_map/reduce_scatter | solution.py:107
  368.2 1.2 copy-start.1
  389.1 28.8 %copy-start.2 = (bf16[384,1152]{1,0:T(8,128)(2,1)S(1)}, bf16[384,1152]{1,0:T(8,128)(2,1)}, u32[]{:S(2)}) copy-start(bf16[384,1152]{1,0:T(8,128)(2,1)} %param.12) | copy-start | bytes 2654212
  419.7 410.8 %reduce-scatter.5.cloned.1.call-start = ((), (), s32[]{:S(2)}) async-start(), calls=%async_computation.11 | async-start | bytes 1216512 | tf_op jit(solution)/shard_map/reduce_scatter | solution.py:107
Sparse Core Ops, SparseCore 0:
  66.6 73.5 all-gather.4
  143.4 79.6 all-gather.6
  244.2 119.2 all-reduce.9
  419.8 199.3 reduce-scatter.2
  624.1 206.3 reduce-scatter.4
where the time goes:
time: 843 us; the launch traced here: 838 us
  waiting for transfers between devices  578 us (69%)
  blocking collectives  190 us (23%)
  starting transfers between devices  19.3 us (2%)
  between operations  14 us (2%)
  local copies, waits for them, and re-layouts  13.5 us (2%)
  other arithmetic  12.6 us (1%)
  matrix products  10.8 us (1%)
    reduce_scatter x2, waiting for transfers between devices, shards(): lax.psum_scatter(jnp.dot(feature_rows, out_weight, preferred_element_type...  367 us
    all_gather x2, waiting for transfers between devices, shards(): lax.all_gather(normed, 'hidden', axis=0, tiled=True)  146 us
    unnamed x1, blocking collectives  52.4 us
    all_to_all x2, blocking collectives, to_feature_rows(): lax.all_to_all(gathered, 'hidden', split_axis=1, concat_axis=0, tiled=True)  42.2 us
    unnamed x6, waiting for transfers between devices  40.3 us
    all_gather x2, blocking collectives, to_feature_rows(): gathered = lax.all_gather(attended, 'width', axis=0, tiled=True)  39.3 us
    psum x1, blocking collectives, normalize(): average = lax.psum(jnp.sum(values, axis=1), 'width') / D  30.6 us
    psum x1, blocking collectives, normalize(): spread = lax.psum(jnp.sum(centered * centered, axis=1), 'width') / D  25.8 us
  transfers between devices with their start and end apart: 9, of which 8 were waited for; matrix products, arithmetic and copies ran while one was open for 2% of the time, Pallas kernels for 0%

commit v1 on v0

v1 whole, which is shorter than its diff:
```python
import jax
import jax.numpy as jnp
from jax import lax
from jax.experimental import pallas as pl
from jax.experimental.pallas import tpu as pltpu
from jax.sharding import PartitionSpec as P

MESH = pl.DeviceIdType.MESH
F32, BF16 = jnp.float32, jnp.bfloat16

D = 18432
HEADS = 48
HEAD_DIM = 256
CACHE = 2048
FEAT_DEV = 384
WIDTH_DEV = 1152
WIDTH_CHIP = 2304
JOINT = 512
EPS = 1e-05
MASKED_SCORE = -1e30

X, Y, Z = 4, 8, 8
CUT = 1024
REST = WIDTH_CHIP - CUT
ORDER = (0, 1, 7, 2, 6, 3, 5, 4)
POS = {ry: pos for pos, ry in enumerate(ORDER)}
BY_DISTANCE = ((0,), (1, 7), (2, 6), (3, 5), (4,))
CHUNKS = ((0, 3), (3, 5), (5, 7), (7, 8))

SENDS = 340
ARRIVALS = 340


class Links:
    def __init__(self, send_sems, recv_sems):
        self.send_sems = send_sems
        self.recv_sems = recv_sems
        self.sent = []
        self.keys = {}
        self.h = lax.axis_index("hidden")
        self.w = lax.axis_index("width")
        self.y, self.x = lax.div(self.h, X), lax.rem(self.h, X)
        self.z, self.c = lax.div(self.w, 2), lax.rem(self.w, 2)

    def hidden(self, ry, rx):
        return lax.rem(self.y + ry, Y) * X + lax.rem(self.x + rx, X)

    def width(self, rz, rc):
        return lax.rem(self.z + rz, Z) * 2 + self.core(rc)

    def core(self, rc):
        return self.c if rc == 0 else 1 - self.c

    def device(self, ry=0, rx=0, rz=0, rc=0):
        return {"hidden": self.hidden(ry % Y, rx % X), "width": self.width(rz % Z, rc)}

    def arrival(self, key):
        return self.recv_sems.at[self.keys.setdefault(key, len(self.keys))]

    def push(self, src, dst, to, key):
        copy = pltpu.make_async_remote_copy(
            src_ref=src,
            dst_ref=dst,
            send_sem=self.send_sems.at[len(self.sent)],
            recv_sem=self.arrival(key),
            device_id=self.device(**to),
            device_id_type=MESH,
        )
        copy.start()
        self.sent.append(copy)

    def arrive(self, dst, key):
        pltpu.make_async_remote_copy(
            src_ref=dst,
            dst_ref=dst,
            send_sem=self.send_sems.at[0],
            recv_sem=self.arrival(key),
            device_id=self.device(rc=1),
            device_id_type=MESH,
        ).wait_recv()

    def finish(self):
        for copy in self.sent:
            copy.wait_send()


def iota(shape, axis):
    return lax.broadcasted_iota(jnp.int32, shape, axis)


def kernel(tokens, gain, lengths, query_weight, keyval_weight, out_weight, key_cache, value_cache, out, s):
    links = Links(s["send_sems"], s["recv_sems"])
    c, z, h, w = links.c, links.z, links.h, links.w
    width_peers = [(rz, rc) for rz in (4, 3, 5, 2, 6, 1, 7, 0) for rc in (0, 1) if (rz, rc) != (0, 0)]
    hidden_peers = [(ry, rx) for ry in reversed(ORDER) for rx in (2, 1, 3, 0) if (ry, rx) != (0, 0)]

    joint, out_w = s["joint"], s["out_w"]
    mine = pl.ds(pl.multiple_of(c * WIDTH_DEV, WIDTH_DEV), WIDTH_DEV)
    local = s["local_sems"]
    loads = [
        pltpu.make_async_copy(keyval_weight, s["keyval_w"], local.at[0]),
        pltpu.make_async_copy(query_weight, joint.at[mine, pl.ds(0, FEAT_DEV)], local.at[1]),
        pltpu.make_async_copy(out_weight, out_w.at[c], local.at[2]),
        pltpu.make_async_copy(key_cache.at[0], s["keys"], local.at[3]),
        pltpu.make_async_copy(value_cache.at[0], s["values"], local.at[4]),
    ]
    for load in loads:
        load.start()

    barrier = pltpu.get_barrier_semaphore()
    for rz, rc in width_peers:
        pl.semaphore_signal(barrier, inc=1, device_id=links.device(rz=rz, rc=rc), device_id_type=MESH)
    for ry, rx in hidden_peers:
        pl.semaphore_signal(barrier, inc=1, device_id=links.device(ry=ry, rx=rx), device_id_type=MESH)

    rows = tokens[...].astype(F32).reshape(32, WIDTH_DEV)
    own_mean = jnp.sum(rows, axis=1, keepdims=True) * (1.0 / WIDTH_DEV)
    centered = rows - own_mean
    own_spread = jnp.sum(centered * centered, axis=1, keepdims=True)
    diagonal = iota((32, 128), 0) == iota((32, 128), 1)
    mean_lanes = jnp.sum(jnp.where(diagonal, own_mean, 0.0), axis=0, keepdims=True)
    spread_lanes = jnp.sum(jnp.where(diagonal, own_spread, 0.0), axis=0, keepdims=True)
    stats = s["stats"]
    stats[0] = jnp.where(iota((8, 128), 0) == 0, mean_lanes, spread_lanes)
    gains = s["gains"]
    gains[c] = jnp.broadcast_to(gain[...], (8, WIDTH_DEV))
    halves = s["halves"]
    halves[c] = tokens[c]

    pl.semaphore_wait(barrier, len(width_peers) + len(hidden_peers))

    for rz, rc in width_peers:
        slot = ((-rz) % Z) * 2 + rc
        links.push(stats.at[0], stats.at[slot], dict(rz=rz, rc=rc), ("stats", slot))
    links.push(tokens.at[1 - c], halves.at[c], dict(rc=1), "halves")
    links.push(gains.at[c], gains.at[c], dict(rc=1), "gains")
    loads[0].wait()
    joint[mine, FEAT_DEV:JOINT] = jnp.concatenate(
        [s["keyval_w"][...], jnp.zeros((WIDTH_DEV, JOINT - FEAT_DEV - 16), BF16)], axis=1
    )
    loads[1].wait()
    links.push(joint.at[mine], joint.at[mine], dict(rc=1), "joint")
    loads[2].wait()

    for rz, rc in width_peers:
        slot = rz * 2 + rc
        links.arrive(stats.at[slot], ("stats", slot))
    gathered = stats[...]
    mean = jnp.sum(gathered, axis=0) * (1.0 / 16)
    apart = gathered - mean[None]
    first = iota((8, 128), 0) == 0
    spread = jnp.sum(jnp.where(first[None], WIDTH_DEV * (apart * apart), gathered), axis=0)
    scale = lax.rsqrt((spread[0:1] + spread[1:2]) * (1.0 / D) + EPS)
    here = iota((16, 128), 1) == iota((16, 128), 0) + c * 16
    row_mean = jnp.sum(jnp.where(here, mean[0:1], 0.0), axis=1, keepdims=True)
    row_scale = jnp.sum(jnp.where(here, scale, 0.0), axis=1, keepdims=True)
    links.arrive(halves.at[1 - c], "halves")
    links.arrive(gains.at[1 - c], "gains")
    normed = [
        ((halves[half].astype(F32) - row_mean) * row_scale * gains[half, 0:1]).astype(BF16) for half in (0, 1)
    ]
    ga, gb = s["ga"], s["gb"]
    ga[0, 0] = normed[0][:, :CUT]
    gb[0, 0] = jnp.concatenate([normed[0][:, CUT:], normed[1]], axis=1)

    def a_along_y(ry, rx, up):
        to = (ry - 1) % Y if up else (ry + 1) % Y
        if to == 4 and up != (rx < 2):
            return
        links.push(ga.at[POS[ry], rx], ga.at[POS[to], rx], dict(ry=1 if up else -1), ("a", to, rx))

    def b_along_y(ry, up):
        to = (ry - 1) % Y if up else (ry + 1) % Y
        if to == 4 and not up:
            return
        links.push(gb.at[POS[ry], 0], gb.at[POS[to], 0], dict(ry=1 if up else -1), ("b", to, 0))

    def b_along_x(ry, rx, right):
        to = (rx - 1) % X if right else (rx + 1) % X
        links.push(gb.at[POS[ry], rx], gb.at[POS[ry], to], dict(rx=1 if right else -1), ("b", ry, to))

    def a_from(ry, rx):
        links.arrive(ga.at[POS[ry], rx], ("a", ry, rx))

    def b_from(ry, rx):
        links.arrive(gb.at[POS[ry], rx], ("b", ry, rx))

    acc, spread_out, packed, shares = s["acc"], s["spread_out"], s["packed"], s["shares"]
    owned, owned_sum, queries = s["owned"], s["owned_sum"], s["queries"]

    def project(chunk):
        p0, p1 = CHUNKS[chunk]
        count = p1 - p0
        if chunk == 0:
            links.arrive(joint.at[pl.ds(pl.multiple_of((1 - c) * WIDTH_DEV, WIDTH_DEV), WIDTH_DEV)], "joint")
        partial = jnp.dot(
            ga[p0:p1].reshape(count * 64, CUT), joint[0:CUT], preferred_element_type=F32
        ) + jnp.dot(gb[p0:p1].reshape(count * 64, REST), joint[CUT:WIDTH_CHIP], preferred_element_type=F32)
        for k in range(4):
            acc[k, p0 * 64 : p1 * 64] = partial[:, k * 128 : (k + 1) * 128]
        span = slice(p0 * 16, p1 * 16)
        for row in range(16):
            for k in range(4):
                spread_out[row, pl.ds(p0 * 16 + k, count * 4, stride=4), :] = acc[
                    k, pl.ds(p0 * 64 + row, count * 4, stride=16), :
                ]
            packed[row, span] = spread_out[row, span].astype(BF16)
        part = pl.ds(p0 * 16, count * 16)
        for rz, rc in width_peers:
            links.push(
                packed.at[links.width(rz, rc), part],
                shares.at[c, (-rz) % Z, part],
                dict(rz=rz, rc=rc),
                ("shares", chunk, (-rz) % Z, rc),
            )
        shares[c, 0, span] = packed[w, span]

    def hand_out(chunk):
        p0, p1 = CHUNKS[chunk]
        count = p1 - p0
        span = slice(p0 * 16, p1 * 16)
        for rz, rc in width_peers:
            links.arrive(shares.at[links.core(rc), rz, pl.ds(p0 * 16, count * 16)], ("shares", chunk, rz, rc))
        for step in range(2):
            total = shares[step, 0, span].astype(F32)
            for rz in range(1, Z):
                total = total + shares[step, rz, span].astype(F32)
            owned_sum[step, span] = total
            for k in range(4):
                owned[pl.ds(p0 * 32 + step * 4 + k, count * 4, stride=8), :] = owned_sum[
                    step, pl.ds(p0 * 16 + k, count * 4, stride=4), :
                ]
        here_h = pl.ds(pl.multiple_of(h * 8, 8), 8)
        for pos in range(p0, p1):
            ry = ORDER[pos]
            for rx in range(X):
                tile = pl.ds((pos * X + rx) * 8, 8)
                if (ry, rx) == (0, 0):
                    queries[here_h] = owned[tile]
                else:
                    links.push(
                        owned.at[tile],
                        queries.at[here_h],
                        dict(ry=ry, rx=rx),
                        ("queries", (-ry) % Y, (-rx) % X),
                    )

    for rx in (1, 3, 2):
        links.push(ga.at[0, 0], ga.at[0, (-rx) % X], dict(rx=rx), ("a", 0, (-rx) % X))
    for up in (True, False):
        b_along_y(0, up)
        a_along_y(0, 0, up)
    for right in (True, False):
        b_along_x(0, 0, right)
    links.push(out_w.at[c], out_w.at[c], dict(rc=1), "out_w")
    for rx in (1, 3, 2):
        a_from(0, rx)
        for up in (True, False):
            a_along_y(0, rx, up)

    def b_second(distance):
        for ry in BY_DISTANCE[distance]:
            b_from(ry, 1)
            if POS[ry] % 2 == 1:
                b_along_x(ry, 1, False)
            b_from(ry, 3)
            if POS[ry] % 2 == 0:
                b_along_x(ry, 3, True)

    def b_third(distance):
        for ry in BY_DISTANCE[distance]:
            b_from(ry, 2)

    for distance in range(1, 5):
        for ry in BY_DISTANCE[distance]:
            b_from(ry, 0)
            if ry >= 5:
                b_along_y(ry, True)
            if ry <= 3:
                b_along_y(ry, False)
            for right in (True, False):
                b_along_x(ry, 0, right)
        b_second(distance - 1)
        for ry in BY_DISTANCE[distance]:
            for rx in range(X):
                a_from(ry, rx)
                if ry >= 5:
                    a_along_y(ry, rx, True)
                if ry <= 3:
                    a_along_y(ry, rx, False)
        if distance >= 2:
            b_third(distance - 2)
        if distance >= 3:
            project(distance - 3)
        if distance >= 4:
            hand_out(distance - 4)
    b_second(4)
    b_third(3)
    project(2)
    hand_out(1)
    b_third(4)
    project(3)
    hand_out(2)
    hand_out(3)

    for ry, rx in hidden_peers:
        links.arrive(
            queries.at[pl.ds(pl.multiple_of(links.hidden(ry, rx) * 8, 8), 8)], ("queries", ry, rx)
        )
    blocks = s["blocks"]
    fresh = []
    lane_of = (iota((128, JOINT), 1) & 15) == iota((128, JOINT), 0)
    group_of = (iota((32, JOINT), 1) >> 4) == iota((32, JOINT), 0)
    for step in range(2):
        for k in range(3):
            blocks[pl.ds(step * 96 + k, 32, stride=3), :] = queries[pl.ds(step * 4 + k, 32, stride=8), :]
        keyval = queries[pl.ds(step * 4 + 3, 32, stride=8), :].astype(BF16)
        copies = jnp.dot(keyval, jnp.where(lane_of, 1.0, 0.0).astype(BF16), preferred_element_type=F32)
        fresh.append(jnp.sum(jnp.where(group_of, copies, 0.0), axis=0, keepdims=True))
    rows128 = iota((128, JOINT), 0)
    fresh_all = jnp.where(rows128 == 0, fresh[0], jnp.where(rows128 == 1, fresh[1], 0.0)).astype(BF16)
    query = jnp.concatenate(
        [
            jnp.concatenate(
                [blocks[pl.ds(step * 96 + half, 48, stride=2), :] for half in (0, 1)], axis=1
            )
            for step in range(2)
        ],
        axis=0,
    ).astype(BF16)
    inv_root = HEAD_DIM ** (-0.5)
    over_keys = (((1,), (1,)), ((), ()))
    loads[3].wait()
    cached = lax.dot_general(query, s["keys"][...], over_keys, preferred_element_type=F32) * inv_root
    cached = jnp.where(iota((96, CACHE), 1) < lengths[0], cached, MASKED_SCORE)
    new = lax.dot_general(query, fresh_all[:, :HEAD_DIM], over_keys, preferred_element_type=F32) * inv_root
    lane, row = iota((96, 128), 1), iota((96, 128), 0)
    new = jnp.where((lane == 0) | ((lane == 1) & (row >= HEADS)), new, MASKED_SCORE)
    peak = jnp.maximum(jnp.max(cached, axis=1, keepdims=True), jnp.max(new, axis=1, keepdims=True))
    cached = jnp.exp(cached - peak)
    new = jnp.exp(new - peak)
    total = jnp.sum(cached, axis=1, keepdims=True) + jnp.sum(new, axis=1, keepdims=True)
    loads[4].wait()
    weighted = jnp.dot(cached.astype(BF16), s["values"][...], preferred_element_type=F32) + jnp.dot(
        new.astype(BF16), fresh_all[:, HEAD_DIM:], preferred_element_type=F32
    )
    attended = (weighted / total).astype(BF16).astype(F32)

    att_blocks, leaving, landed = s["att_blocks"], s["leaving"], s["landed"]
    for step in range(2):
        for half in (0, 1):
            att_blocks[pl.ds(step * 96 + half, 48, stride=2), :] = attended[
                step * 48 : (step + 1) * 48, half * 128 : (half + 1) * 128
            ]
        for k in range(3):
            leaving[pl.ds(step * 4 + k, 32, stride=8), :] = att_blocks[pl.ds(step * 96 + k, 32, stride=3), :]
        leaving[pl.ds(step * 4 + 3, 32, stride=8), :] = jnp.zeros((32, 128), F32)
    for ry, rx in hidden_peers:
        slot = POS[(-ry) % Y] * X + (-rx) % X
        links.push(
            leaving.at[pl.ds(pl.multiple_of(links.hidden(ry, rx) * 8, 8), 8)],
            landed.at[pl.ds(slot * 8, 8)],
            dict(ry=ry, rx=rx),
            ("landed", slot),
        )
    landed[0:8] = leaving[pl.ds(pl.multiple_of(h * 8, 8), 8)]

    along_f32, along, whole, whole_f32 = s["along_f32"], s["along"], s["whole"], s["whole_f32"]
    feature_rows, product = s["feature_rows"], s["product"]

    def pass_along(chunk):
        p0, p1 = CHUNKS[chunk]
        count = p1 - p0
        span = slice(p0 * 16, p1 * 16)
        part = pl.ds(p0 * 16, count * 16)
        for slot in range(max(p0 * X, 1), p1 * X):
            links.arrive(landed.at[pl.ds(slot * 8, 8)], ("landed", slot))
        for step in range(2):
            for k in range(4):
                along_f32[step, pl.ds(p0 * 16 + k, count * 4, stride=4), :] = landed[
                    pl.ds(p0 * 32 + step * 4 + k, count * 4, stride=8), :
                ]
            along[step, span] = along_f32[step, span].astype(BF16)
        for rz, rc in width_peers:
            links.push(
                along.at[links.core(rc), part],
                whole.at[w, part],
                dict(rz=rz, rc=rc),
                ("whole", chunk, (-rz) % Z, rc),
            )
        whole[w, span] = along[c, span]

    def multiply(chunk):
        p0, p1 = CHUNKS[chunk]
        count = p1 - p0
        span = slice(p0 * 16, p1 * 16)
        for rz, rc in width_peers:
            links.arrive(whole.at[links.width(rz, rc), pl.ds(p0 * 16, count * 16)], ("whole", chunk, rz, rc))
        for row in range(16):
            whole_f32[row, span] = whole[row, span].astype(F32)
            for k in range(3):
                feature_rows[k, pl.ds(p0 * 64 + row, count * 4, stride=16), :] = whole_f32[
                    row, pl.ds(p0 * 16 + k, count * 4, stride=4), :
                ]
        if chunk == 3:
            links.arrive(out_w.at[1 - c], "out_w")
        operand = jnp.concatenate([feature_rows[k, p0 * 64 : p1 * 64] for k in range(3)], axis=1).astype(BF16)
        for half in (0, 1):
            product[p0 * 64 : p1 * 64, half * WIDTH_DEV : (half + 1) * WIDTH_DEV] = jnp.dot(
                operand, out_w[half], preferred_element_type=F32
            )

    sa, sb, la, lax_, lbx, lby = s["sa"], s["sb"], s["la"], s["lax"], s["lbx"], s["lby"]

    def own_a(ry, rx):
        at = (POS[ry] * X + rx) * 16
        return product[at : at + 16, 0:CUT]

    def own_b(ry, rx):
        at = (POS[ry] * X + rx) * 16
        return product[at : at + 16, CUT:WIDTH_CHIP]

    def y_slot(ry, up):
        return 8 if ry == 0 and not up else POS[ry]

    def from_y(buffer, name, ry, rx, up):
        slot = buffer.at[y_slot(ry, up), rx]
        links.arrive(slot, (name, ry, rx, up))
        return slot[...].astype(F32)

    def to_y(name, source, buffer, ry, rx, up):
        to = ry - 1 if up else (ry + 1) % Y
        links.push(source, buffer.at[y_slot(to, up), rx], dict(ry=1 if up else -1), (name, to, rx, up))

    def a_sums(distance):
        for ry in BY_DISTANCE[distance]:
            for rx in range(X):
                if ry == 4:
                    up = rx < 2
                else:
                    up = ry <= 3
                total = own_a(ry, rx)
                if distance in (1, 2) or (distance == 3 and up == (rx < 2)):
                    total = total + from_y(la, "la", ry, rx, up)
                sa[POS[ry], rx] = total.astype(BF16)
                to_y("la", sa.at[POS[ry], rx], la, ry, rx, up)

    def a_rows():
        for rx in (2, 1, 3):
            total = own_a(0, rx) + from_y(la, "la", 0, rx, True) + from_y(la, "la", 0, rx, False)
            sa[0, rx] = total.astype(BF16)
            links.push(sa.at[0, rx], lax_.at[rx - 1], dict(rx=rx), ("lax", rx))

    def from_x(ry, slot):
        links.arrive(lbx.at[POS[ry], slot], ("lbx", ry, slot))
        return lbx[POS[ry], slot].astype(F32)

    def to_x(ry, rx, slot, right):
        links.push(sb.at[POS[ry], rx], lbx.at[POS[ry], slot], dict(rx=1 if right else -1), ("lbx", ry, slot))

    def b_far(distance):
        for ry in BY_DISTANCE[distance]:
            right = POS[ry] % 2 == 0
            sb[POS[ry], 2] = own_b(ry, 2).astype(BF16)
            to_x(ry, 2, 1 if right else 3, right)

    def b_near(distance):
        for ry in BY_DISTANCE[distance]:
            for rx in (1, 3):
                total = own_b(ry, rx)
                if (rx == 1) == (POS[ry] % 2 == 0):
                    total = total + from_x(ry, rx)
                sb[POS[ry], rx] = total.astype(BF16)
                to_x(ry, rx, 0 if rx == 1 else 2, rx == 1)

    def b_column(ry):
        return own_b(ry, 0) + from_x(ry, 0) + from_x(ry, 2)

    def b_sums(distance):
        for ry in BY_DISTANCE[distance]:
            up = ry <= 4
            total = b_column(ry)
            if distance in (1, 2) or ry == 3:
                total = total + from_y(lby, "lby", ry, 0, up)
            sb[POS[ry], 0] = total.astype(BF16)
            to_y("lby", sb.at[POS[ry], 0], lby, ry, 0, up)

    for chunk in (3, 2, 1, 0):
        pass_along(chunk)
    for turn in range(7):
        if turn < 4:
            multiply(3 - turn)
        distance = 4 - turn
        if distance >= 1:
            a_sums(distance)
        if distance == 0:
            a_rows()
        if distance >= 0:
            b_far(distance)
        if 0 <= distance + 1 <= 4:
            b_near(distance + 1)
        if 1 <= distance + 2 <= 4:
            b_sums(distance + 2)
    last_a = own_a(0, 0) + from_y(la, "la", 0, 0, True) + from_y(la, "la", 0, 0, False)
    for rx in (1, 3, 2):
        links.arrive(lax_.at[rx - 1], ("lax", rx))
        last_a = last_a + lax_[rx - 1].astype(F32)
    last_b = b_column(0) + from_y(lby, "lby", 0, 0, True) + from_y(lby, "lby", 0, 0, False)
    done = jnp.concatenate([last_a, last_b], axis=1).astype(BF16)
    result, swapped = s["result"], s["swapped"]
    for half in (0, 1):
        result[half] = done[:, half * WIDTH_DEV : (half + 1) * WIDTH_DEV]
    links.push(result.at[1 - c], swapped.at[c], dict(rc=1), "swapped")
    out[c] = result[c]
    links.arrive(swapped.at[1 - c], "swapped")
    out[1 - c] = swapped[1 - c]
    links.finish()
    assert len(links.sent) <= SENDS and len(links.keys) <= ARRIVALS


SCRATCH = dict(
    stats=((16, 8, 128), F32),
    gains=((2, 8, WIDTH_DEV), F32),
    halves=((2, 16, WIDTH_DEV), BF16),
    joint=((WIDTH_CHIP, JOINT), BF16),
    keyval_w=((WIDTH_DEV, 16), BF16),
    out_w=((2, FEAT_DEV, WIDTH_DEV), BF16),
    keys=((CACHE, HEAD_DIM), BF16),
    values=((CACHE, HEAD_DIM), BF16),
    ga=((Y, X, 16, CUT), BF16),
    gb=((Y, X, 16, REST), BF16),
    acc=((4, 512, 128), F32),
    spread_out=((16, 128, 128), F32),
    packed=((16, 128, 128), BF16),
    shares=((2, Z, 128, 128), BF16),
    owned_sum=((2, 128, 128), F32),
    owned=((256, 128), F32),
    queries=((256, 128), F32),
    blocks=((192, 128), F32),
    att_blocks=((192, 128), F32),
    leaving=((256, 128), F32),
    landed=((256, 128), F32),
    along_f32=((2, 128, 128), F32),
    along=((2, 128, 128), BF16),
    whole=((16, 128, 128), BF16),
    whole_f32=((16, 128, 128), F32),
    feature_rows=((3, 512, 128), F32),
    product=((512, WIDTH_CHIP), F32),
    sa=((Y, X, 16, CUT), BF16),
    sb=((Y, X, 16, REST), BF16),
    la=((Y + 1, X, 16, CUT), BF16),
    lax=((3, 16, CUT), BF16),
    lbx=((Y, X, 16, REST), BF16),
    lby=((Y + 1, 1, 16, REST), BF16),
    result=((2, 16, WIDTH_DEV), BF16),
    swapped=((2, 16, WIDTH_DEV), BF16),
)


def shards(tokens, gain, query_weight, keyval_weight, out_weight, key_cache, value_cache, lengths):
    names = list(SCRATCH)

    def body(*refs):
        scratch = dict(zip(names, refs[9:]))
        scratch.update(send_sems=refs[-3], recv_sems=refs[-2], local_sems=refs[-1])
        kernel(*refs[:9], scratch)

    vmem, smem, hbm = (pl.BlockSpec(memory_space=space) for space in (pltpu.VMEM, pltpu.SMEM, pl.ANY))
    return pl.pallas_call(
        body,
        out_shape=jax.ShapeDtypeStruct(tokens.shape, BF16),
        in_specs=[vmem, vmem, smem, hbm, hbm, hbm, hbm, hbm],
        out_specs=vmem,
        scratch_shapes=[pltpu.VMEM(shape, dtype) for shape, dtype in SCRATCH.values()]
        + [
            pltpu.SemaphoreType.DMA((SENDS,)),
            pltpu.SemaphoreType.DMA((ARRIVALS,)),
            pltpu.SemaphoreType.DMA((5,)),
        ],
        compiler_params=pltpu.CompilerParams(
            collective_id=0, has_side_effects=True, vmem_limit_bytes=48 * 1024 * 1024
        ),
    )(tokens, gain.reshape(1, -1), lengths, query_weight, keyval_weight, out_weight, key_cache, value_cache)


def solution(mesh):
    return jax.shard_map(
        shards,
        mesh=mesh,
        in_specs=(
            P(None, "hidden", "width"),
            P("width"),
            P("width", "hidden"),
            P("width", "hidden"),
            P("hidden", "width"),
            P(("hidden", "width"), None, None),
            P(("hidden", "width"), None, None),
            P(("hidden", "width")),
        ),
        out_specs=P(None, "hidden", "width"),
        check_vma=False,
    )
```

time: 843 us -> 114 us (0.14)
  waiting for transfers between devices: 578 us -> 0 us
  blocking collectives: 190 us -> 0 us
  Pallas kernels: 0 us -> 106 us
  starting transfers between devices: 19.3 us -> 0 us
  between operations: 14 us -> 0.68 us
  other arithmetic: 12.6 us -> 0 us
  matrix products: 10.8 us -> 0 us
    reduce_scatter x2 -> x0, waiting for transfers between devices: 367 us -> none  [shards(): lax.psum_scatter(jnp.dot(feature_rows, out_weight, preferred_element_type...]
    all_gather x2 -> x0, waiting for transfers between devices: 146 us -> none  [shards(): lax.all_gather(normed, 'hidden', axis=0, tiled=True)]
    pallas_call x0 -> x1, Pallas kernels: none -> 106 us  [shards(): pl.pallas_call(body, out_shape=jax.ShapeDtypeStruct(tokens.shape, BF16),...]
    psum x2 -> x0, blocking collectives: 56.4 us -> none  [the longest x1 30.6 us: normalize(): average = lax.psum(jnp.sum(values, axis=1), 'width') / D]
    unnamed x1 -> x0, blocking collectives: 52.4 us -> none
    all_to_all x2 -> x0, blocking collectives: 42.2 us -> none  [to_feature_rows(): lax.all_to_all(gathered, 'hidden', split_axis=1, concat_axis=0, tiled=True)]
    unnamed x6 -> x0, waiting for transfers between devices: 40.3 us -> none
    all_gather x2 -> x0, blocking collectives: 39.3 us -> none  [to_feature_rows(): gathered = lax.all_gather(attended, 'width', axis=0, tiled=True)]
  transfers between devices with their start and end apart: 9 -> 0, of which waited for: 8 -> 0; matrix products, arithmetic and copies ran while one was open for 2% -> 0% of each run, Pallas kernels for 0% -> 0%
where the time goes in v1:
time: 114 us
  Pallas kernels  106 us (93%)
  local copies, waits for them, and re-layouts  7.13 us (6%)
    pallas_call x1, Pallas kernels, shards(): pl.pallas_call(body, out_shape=jax.ShapeDtypeStruct(tokens.shape, BF16),...  106 us
    unnamed x12, local copies, waits for them, and re-layouts  6.43 us

profile of v1, /device:TPU:1, one launch (start us, length us, event | category | flops | bytes accessed | tf_op | source)
XLA Modules:
  0.0 113.8 jit_solution(3698231620071177165)
XLA Ops:
  0.7 0.7 reshape.3.refs_1_
  1.4 0.0 copy-start.4
  1.4 1.0 copy.9.refs_4_
  2.4 0.0 copy-done.4
  2.4 0.0 copy-start
  2.4 1.2 %copy-done = bf16[1,2048,256]{2,1,0:T(8,128)(2,1)S(1)} copy-done((bf16[1,2048,256]{2,1,0:T(8,128)(2,1)S(1)}, bf16[1,2048,256]{2,1,0:T(8,128)(2,1)}, u32[]{:S(2)}) %copy-start) | copy-done | bytes 1048600
  3.6 0.0 copy-start.1
  3.6 1.2 %copy-done.1 = bf16[1,2048,256]{2,1,0:T(8,128)(2,1)S(1)} copy-done((bf16[1,2048,256]{2,1,0:T(8,128)(2,1)S(1)}, bf16[1,2048,256]{2,1,0:T(8,128)(2,1)}, u32[]{:S(2)}) %copy-start.1) | copy-done | bytes 1048600
  4.8 0.0 copy-start.2
  4.8 1.2 %copy-done.2 = bf16[1152,384]{1,0:T(8,128)(2,1)S(1)} copy-done((bf16[1152,384]{1,0:T(8,128)(2,1)S(1)}, bf16[1152,384]{1,0:T(8,128)(2,1)}, u32[]{:S(2)}) %copy-start.2) | copy-done | bytes 884760
  6.0 0.0 copy-start.3
  6.0 1.2 %copy-done.3 = bf16[384,1152]{1,0:T(8,128)(2,1)S(1)} copy-done((bf16[384,1152]{1,0:T(8,128)(2,1)S(1)}, bf16[384,1152]{1,0:T(8,128)(2,1)}, u32[]{:S(2)}) %copy-start.3) | copy-done | bytes 884760
  7.2 106.0 %shard_map.82 = bf16[2,16,1152]{2,1,0:T(8,128)(2,1)S(1)} custom-call(bf16[2,16,1152]{2,1,0:T(8,128)(2,1)S(1)} %copy-done.4, f32[1,1152]{1,0:T(1,128)S(1)} %reshape.3.refs_1_, s32[1]{0:T(128)S(6)} %copy.11.refs_2_, bf16[1152,384]{1,0:T(8,128)(2,1)S(1)} %copy-done.2, bf16[1152,16]{1,0:T(8,128)(2,1)S(1)} %copy.9.refs_4_, bf16[384,1152]{1,0:T(8,128)(2,1)S(1)} %copy-done.3, ...), custom_call_target="tpu_custom_call" | custom-call | tf_op jit(solution)/shard_map/pallas_call | solution.py:569
  113.2 0.6 copy.12
Async XLA Ops:
  1.4 1.0 copy-start.4
  2.4 1.2 %copy-start = (bf16[1,2048,256]{2,1,0:T(8,128)(2,1)S(1)}, bf16[1,2048,256]{2,1,0:T(8,128)(2,1)}, u32[]{:S(2)}) copy-start(bf16[1,2048,256]{2,1,0:T(8,128)(2,1)} %refs_6_.1) | copy-start | bytes 3145732
  3.6 1.2 %copy-start.1 = (bf16[1,2048,256]{2,1,0:T(8,128)(2,1)S(1)}, bf16[1,2048,256]{2,1,0:T(8,128)(2,1)}, u32[]{:S(2)}) copy-start(bf16[1,2048,256]{2,1,0:T(8,128)(2,1)} %refs_7_.1) | copy-start | bytes 3145732
  4.8 1.2 %copy-start.2 = (bf16[1152,384]{1,0:T(8,128)(2,1)S(1)}, bf16[1152,384]{1,0:T(8,128)(2,1)}, u32[]{:S(2)}) copy-start(bf16[1152,384]{1,0:T(8,128)(2,1)} %refs_3_.1) | copy-start | bytes 2654212
  6.0 1.2 %copy-start.3 = (bf16[384,1152]{1,0:T(8,128)(2,1)S(1)}, bf16[384,1152]{1,0:T(8,128)(2,1)}, u32[]{:S(2)}) copy-start(bf16[384,1152]{1,0:T(8,128)(2,1)} %refs_5_.1) | copy-start | bytes 2654212

commit v2 on v1

v2 whole, which is shorter than its diff:
```python
import jax
import jax.numpy as jnp
from jax import lax
from jax.experimental import pallas as pl
from jax.experimental.pallas import tpu as pltpu
from jax.sharding import PartitionSpec as P

MESH = pl.DeviceIdType.MESH
F32, BF16 = jnp.float32, jnp.bfloat16

D = 18432
HEADS = 48
HEAD_DIM = 256
CACHE = 2048
FEAT_DEV = 384
WIDTH_DEV = 1152
WIDTH_CHIP = 2304
JOINT = 512
EPS = 1e-05
MASKED_SCORE = -1e30

X, Y, Z = 4, 8, 8
CUT = 1024
REST = WIDTH_CHIP - CUT
ORDER = (0, 1, 7, 2, 6, 3, 5, 4)
POS = {ry: pos for pos, ry in enumerate(ORDER)}
CHUNKS = ((0, 3), (3, 5), (5, 7), (7, 8))
HALVES = ((0, 4), (4, 8))
STAT = 16

VMEM_BYTES = 60 * 1024 * 1024
ARRIVALS = 144
ARRIVAL_ORDER = (
    ("b", 7, 0), ("b", 1, 0), ("b", 0, 3), ("b", 0, 1), ("a", 0, 3), ("a", 0, 1),
    ("b", 6, 0), ("b", 2, 0), ("a", 7, 0), ("a", 1, 0), ("a", 0, 2), ("b", 7, 3),
    ("b", 7, 1), ("a", 7, 3), ("a", 1, 3), ("b", 1, 3), ("b", 1, 1), ("a", 7, 1),
    ("a", 1, 1), ("b", 0, 2), ("b", 5, 0), ("b", 6, 1), ("b", 3, 0), ("b", 6, 3),
    ("a", 6, 0), ("a", 2, 0), ("b", 2, 1), ("b", 2, 3), ("a", 7, 2), ("a", 1, 2),
    ("a", 6, 3), ("a", 2, 3), ("b", 1, 2), ("b", 7, 2), ("a", 6, 1), ("a", 2, 1),
    ("b", 4, 0), ("b", 5, 3), ("b", 5, 1), ("a", 3, 0), ("a", 5, 0), ("b", 3, 3),
    ("b", 3, 1), ("a", 2, 2), ("a", 6, 2), ("a", 3, 3), ("b", 6, 2), ("b", 2, 2),
    ("a", 5, 3), ("a", 3, 1), ("a", 5, 1), ("b", 4, 3), ("b", 4, 1), ("a", 4, 0),
    ("a", 3, 2), ("b", 3, 2), ("a", 5, 2), ("a", 4, 3), ("a", 4, 1), ("b", 4, 2),
    ("b", 5, 2), ("a", 4, 2),
)


def forwards(part, ry, rx):
    if part == "a":
        along = [(1, 0), (-1, 0)] if ry == 0 else []
        if ry >= 6 or (ry == 5 and rx < 2):
            along = [(1, 0)]
        if ry in (1, 2) or (ry == 3 and rx >= 2):
            along = [(-1, 0)]
        return along + ([(0, 1), (0, -1), (0, 2)] if (ry, rx) == (0, 0) else [])
    if rx == 0:
        along = {0: [(1, 0), (-1, 0), (2, 0), (-2, 0)], 6: [(1, 0)], 5: [(1, 0)], 2: [(-1, 0)]}.get(ry, [])
        return along + [(0, 1), (0, -1)] + ([(0, 2)] if ry == 4 else [])
    if ry != 4 and rx == (3 if POS[ry] % 2 == 0 else 1):
        return [(0, 1 if rx == 3 else -1)]
    return []


def reached(part, ry, rx):
    return [(dy, dx, (part, (ry - dy) % Y, (rx - dx) % X)) for dy, dx in forwards(part, ry, rx)]


BEFORE = {
    key: (-dy, -dx)
    for part in "ab"
    for ry in range(Y)
    for rx in range(X)
    for dy, dx, key in reached(part, ry, rx)
}


class Links:
    def __init__(self, send_sem, recv_sems):
        self.send_sem = send_sem
        self.recv_sems = recv_sems
        self.sent = []
        self.keys = {}
        self.devices = {}
        self.h = lax.axis_index("hidden")
        self.w = lax.axis_index("width")
        self.y, self.x = lax.div(self.h, X), lax.rem(self.h, X)
        self.z, self.c = lax.div(self.w, 2), lax.rem(self.w, 2)

    def hidden(self, ry, rx):
        return lax.rem(self.y + ry % Y, Y) * X + lax.rem(self.x + rx % X, X)

    def width(self, rz, rc):
        return lax.rem(self.z + rz % Z, Z) * 2 + self.core(rc)

    def core(self, rc):
        return self.c if rc == 0 else 1 - self.c

    def device(self, ry=0, rx=0, rz=0, rc=0):
        at = (ry % Y, rx % X, rz % Z, rc)
        if at not in self.devices:
            self.devices[at] = {"hidden": self.hidden(*at[:2]), "width": self.width(*at[2:])}
        return self.devices[at]

    def arrival(self, key):
        return self.recv_sems.at[self.keys.setdefault(key, len(self.keys))]

    def push(self, src, dst, to, key):
        copy = pltpu.make_async_remote_copy(
            src_ref=src,
            dst_ref=dst,
            send_sem=self.send_sem.at[0],
            recv_sem=self.arrival(key),
            device_id=self.device(**to),
            device_id_type=MESH,
        )
        copy.start()
        self.sent.append(copy)

    def arrive(self, dst, key):
        pltpu.make_async_remote_copy(
            src_ref=dst,
            dst_ref=dst,
            send_sem=self.send_sem.at[0],
            recv_sem=self.arrival(key),
            device_id=self.device(rc=1),
            device_id_type=MESH,
        ).wait_recv()

    def finish(self):
        for copy in self.sent:
            copy.wait_send()


def iota(shape, axis):
    return lax.broadcasted_iota(jnp.int32, shape, axis)


def pieces(values):
    high = values.astype(BF16)
    rest = values - high.astype(F32)
    middle = rest.astype(BF16)
    return high, middle, (rest - middle.astype(F32)).astype(BF16)


def sum_all(terms):
    total = terms[0]
    for term in terms[1:]:
        total = total + term
    return total


def kernel(tokens, gain, lengths, query_weight, keyval_weight, out_weight, key_cache, value_cache, out, s):
    links = Links(s["send_sem"], s["recv_sems"])
    c, h, w = links.c, links.h, links.w
    width_peers = [(rz, rc) for rz in (4, 3, 5, 2, 6, 1, 7, 0) for rc in (0, 1) if (rz, rc) != (0, 0)]
    hidden_peers = [(ry, rx) for ry in reversed(ORDER) for rx in (2, 1, 3, 0) if (ry, rx) != (0, 0)]

    barrier = pltpu.get_barrier_semaphore()
    for rz, rc in width_peers:
        pl.semaphore_signal(barrier, inc=1, device_id=links.device(rz=rz, rc=rc), device_id_type=MESH)
    for ry, rx in hidden_peers:
        pl.semaphore_signal(barrier, inc=1, device_id=links.device(ry=ry, rx=rx), device_id_type=MESH)

    joint, out_w = s["joint"], s["out_w"]
    mine = pl.ds(pl.multiple_of(c * WIDTH_DEV, WIDTH_DEV), WIDTH_DEV)
    others = pl.ds(pl.multiple_of((1 - c) * WIDTH_DEV, WIDTH_DEV), WIDTH_DEV)
    local = s["local_sems"]
    loads = [
        pltpu.make_async_copy(keyval_weight, s["keyval_w"], local.at[0]),
        pltpu.make_async_copy(query_weight, joint.at[mine, pl.ds(0, FEAT_DEV)], local.at[1]),
        pltpu.make_async_copy(out_weight, out_w.at[c], local.at[2]),
        pltpu.make_async_copy(key_cache.at[0], s["keys"], local.at[3]),
        pltpu.make_async_copy(value_cache.at[0], s["values"], local.at[4]),
    ]
    for load in loads:
        load.start()

    gain_row = gain[...][None]
    rows = tokens[...].astype(F32).reshape(32, WIDTH_DEV)
    own_mean = jnp.sum(rows, axis=1, keepdims=True) * (1.0 / WIDTH_DEV)
    centered = rows - own_mean
    own_spread = jnp.sum(centered * centered, axis=1, keepdims=True)
    lane = iota((32, 128), 1) - (STAT + 8 * c)
    lanes = jnp.zeros((32, 128), F32)
    for at, piece in enumerate(pieces(own_mean) + pieces(own_spread)):
        lanes = jnp.where(lane == at, piece.astype(F32), lanes)
    own_rows, both = s["own_rows"], s["both"]
    own_rows[...] = jnp.concatenate([centered * gain_row, lanes], axis=1).astype(BF16).reshape(2, 16, WIDTH_DEV + 128)
    both[c] = own_rows[c]

    pl.semaphore_wait(barrier, len(width_peers) + len(hidden_peers))
    links.push(own_rows.at[1 - c], both.at[c], dict(rc=1), "both")

    ga, gb = s["ga"], s["gb"]
    block = {"a": ga, "b": gb}

    def pass_on(part, ry, rx):
        for dy, dx, key in reached(part, ry, rx):
            links.push(
                block[part].at[POS[ry], rx], block[part].at[POS[key[1]], key[2]], dict(ry=dy, rx=dx), key
            )

    links.arrive(both.at[1 - c], "both")
    ga[0, 0] = both[0, :, :CUT]
    gb[0, 0] = jnp.concatenate(
        [both[0, :, CUT:WIDTH_DEV], both[1, :, :WIDTH_DEV], both[0, :, WIDTH_DEV:] + both[1, :, WIDTH_DEV:]], axis=1
    )
    pass_on("b", 0, 0)
    pass_on("a", 0, 0)

    loads[0].wait()
    across = jnp.concatenate([s["keyval_w"][...].astype(F32), jnp.zeros((112, WIDTH_DEV), F32)], axis=0)
    joint[mine, FEAT_DEV:JOINT] = across.T.astype(BF16)
    loads[1].wait()
    links.push(joint.at[mine], joint.at[mine], dict(rc=1), "joint")
    eighth = iota((8, WIDTH_DEV), 0)
    gain_rows = jnp.zeros((8, WIDTH_DEV), F32)
    for at, piece in enumerate(pieces(gain_row)):
        gain_rows = jnp.where(eighth == at, piece.astype(F32), gain_rows)
    weight_sum = jnp.sum(
        jnp.dot(gain_rows.astype(BF16), joint[mine, :], preferred_element_type=F32), axis=0, keepdims=True
    )
    weight_sums = s["weight_sums"]
    eighth = iota((8, 128), 0)
    weight_tile = jnp.zeros((8, 128), F32)
    for k in range(4):
        weight_tile = jnp.where(eighth == k, weight_sum[:, k * 128 : (k + 1) * 128], weight_tile)
    weight_sums[c] = weight_tile
    for rz, rc in width_peers:
        links.push(weight_sums.at[c], weight_sums.at[((-rz) % Z) * 2 + c], dict(rz=rz, rc=rc), "weight_sums")
    loads[2].wait()
    links.push(out_w.at[c], out_w.at[c], dict(rc=1), "out_w")

    acc, spread_out, packed, shares = s["acc"], s["spread_out"], s["packed"], s["shares"]
    each, total, owned, queries = s["each"], s["total"], s["owned"], s["queries"]

    def project(chunk):
        p0, p1 = CHUNKS[chunk]
        count = p1 - p0
        if chunk == 0:
            links.arrive(joint.at[others], "joint")
        stretch = gb[p0:p1].reshape(count * 64, REST + 128)
        partial = jnp.dot(
            ga[p0:p1].reshape(count * 64, CUT), joint[0:CUT], preferred_element_type=F32
        ) + jnp.dot(stretch[:, :REST], joint[CUT:WIDTH_CHIP], preferred_element_type=F32)
        for k in range(4):
            columns = partial[:, k * 128 : (k + 1) * 128]
            acc[k, p0 * 64 : p1 * 64] = columns if k < 3 else columns + stretch[:, REST:].astype(F32)
        span = slice(p0 * 16, p1 * 16)
        for row in range(16):
            for k in range(4):
                spread_out[row, pl.ds(p0 * 16 + k, count * 4, stride=4), :] = acc[
                    k, pl.ds(p0 * 64 + row, count * 4, stride=16), :
                ]
            packed[row, span] = spread_out[row, span].astype(BF16)
        part = pl.ds(p0 * 16, count * 16)
        for rz, rc in width_peers:
            links.push(
                packed.at[links.width(rz, rc), part],
                shares.at[c * Z + (-rz) % Z, part],
                dict(rz=rz, rc=rc),
                ("shares", chunk),
            )
        shares[c * Z, span] = packed[w, span]

    def hand_out(chunk):
        p0, p1 = CHUNKS[chunk]
        count = (p1 - p0) * 4
        span = slice(p0 * 16, p1 * 16)
        links.arrive(shares.at[pl.ds(0, 15), pl.ds(p0 * 16, (p1 - p0) * 16)], ("shares", chunk))
        if chunk == 0:
            links.arrive(weight_sums.at[pl.ds(0, 15)], "weight_sums")
        lane = iota((count, 128), 1) - STAT

        def picked(values, chosen):
            return jnp.sum(jnp.where(chosen, values, 0.0), axis=1, keepdims=True)

        for step in range(2):
            terms = [shares[step * Z + rz, span].astype(F32) for rz in range(Z)]
            for rz in range(Z):
                each[rz, span] = terms[rz]
            total[span] = sum_all(terms)
            means = []
            for rz in range(Z):
                stats = each[rz, pl.ds(p0 * 16 + 3, count, stride=4), :]
                means += [picked(stats, (lane >= first) & (lane < first + 3)) for first in (0, 8)]
            spread = picked(
                total[pl.ds(p0 * 16 + 3, count, stride=4), :],
                ((lane >= 3) & (lane < 6)) | ((lane >= 11) & (lane < 14)),
            )
            mean = sum_all(means) * (1.0 / 16)
            apart = [own - mean for own in means]
            spread = spread + WIDTH_DEV * sum_all([gap * gap for gap in apart])
            scale = lax.rsqrt(spread * (1.0 / D) + EPS)
            for k in range(4):
                values = total[pl.ds(p0 * 16 + k, count, stride=4), :]
                for at, gap in enumerate(apart):
                    values = values + gap * weight_sums[at, k : k + 1, :]
                owned[pl.ds(p0 * 32 + step * 4 + k, count, stride=8), :] = values * scale
        here_h = pl.ds(pl.multiple_of(h * 8, 8), 8)
        for pos in range(p0, p1):
            ry = ORDER[pos]
            for rx in range(X):
                tile = pl.ds((pos * X + rx) * 8, 8)
                if (ry, rx) == (0, 0):
                    queries[here_h] = owned[tile]
                else:
                    links.push(owned.at[tile], queries.at[here_h], dict(ry=ry, rx=rx), "queries")

    missing = [{key for key in ARRIVAL_ORDER if p0 <= POS[key[1]] < p1} for p0, p1 in CHUNKS]
    waiting = []
    for key in ARRIVAL_ORDER:
        part, ry, rx = key
        links.arrive(block[part].at[POS[ry], rx], key)
        pass_on(*key)
        for chunk in range(len(CHUNKS)):
            if key in missing[chunk]:
                missing[chunk].discard(key)
                if not missing[chunk]:
                    project(chunk)
                    if waiting:
                        hand_out(waiting.pop(0))
                    waiting.append(chunk)
    for chunk in waiting:
        hand_out(chunk)

    links.arrive(queries.at[pl.ds(0, 31 * 8)], "queries")
    blocks = s["blocks"]
    fresh = []
    lane_of = (iota((128, JOINT), 1) & 15) == iota((128, JOINT), 0)
    group_of = (iota((32, JOINT), 1) >> 4) == iota((32, JOINT), 0)
    for step in range(2):
        for k in range(3):
            blocks[pl.ds(step * 96 + k, 32, stride=3), :] = queries[pl.ds(step * 4 + k, 32, stride=8), :]
        keyval = queries[pl.ds(step * 4 + 3, 32, stride=8), :].astype(BF16)
        copies = jnp.dot(keyval, jnp.where(lane_of, 1.0, 0.0).astype(BF16), preferred_element_type=F32)
        fresh.append(jnp.sum(jnp.where(group_of, copies, 0.0), axis=0, keepdims=True))
    rows128 = iota((128, JOINT), 0)
    fresh_all = jnp.where(rows128 == 0, fresh[0], jnp.where(rows128 == 1, fresh[1], 0.0)).astype(BF16)
    query = jnp.concatenate(
        [
            jnp.concatenate(
                [blocks[pl.ds(step * 96 + half, 48, stride=2), :] for half in (0, 1)], axis=1
            )
            for step in range(2)
        ],
        axis=0,
    ).astype(BF16)
    inv_root = HEAD_DIM ** (-0.5)
    over_keys = (((1,), (1,)), ((), ()))
    loads[3].wait()
    cached = lax.dot_general(query, s["keys"][...], over_keys, preferred_element_type=F32) * inv_root
    cached = jnp.where(iota((96, CACHE), 1) < lengths[0], cached, MASKED_SCORE)
    new = lax.dot_general(query, fresh_all[:, :HEAD_DIM], over_keys, preferred_element_type=F32) * inv_root
    lane, row = iota((96, 128), 1), iota((96, 128), 0)
    new = jnp.where((lane == 0) | ((lane == 1) & (row >= HEADS)), new, MASKED_SCORE)
    peak = jnp.maximum(jnp.max(cached, axis=1, keepdims=True), jnp.max(new, axis=1, keepdims=True))
    cached = jnp.exp(cached - peak)
    new = jnp.exp(new - peak)
    total = jnp.sum(cached, axis=1, keepdims=True) + jnp.sum(new, axis=1, keepdims=True)
    loads[4].wait()
    weighted = jnp.dot(cached.astype(BF16), s["values"][...], preferred_element_type=F32) + jnp.dot(
        new.astype(BF16), fresh_all[:, HEAD_DIM:], preferred_element_type=F32
    )
    attended = (weighted / total).astype(BF16).astype(F32)

    att_blocks, leaving, landed = s["att_blocks"], s["leaving"], s["landed"]
    for step in range(2):
        for half in (0, 1):
            att_blocks[pl.ds(step * 96 + half, 48, stride=2), :] = attended[
                step * 48 : (step + 1) * 48, half * 128 : (half + 1) * 128
            ]
        for k in range(3):
            leaving[pl.ds(step * 4 + k, 32, stride=8), :] = att_blocks[pl.ds(step * 96 + k, 32, stride=3), :]
        leaving[pl.ds(step * 4 + 3, 32, stride=8), :] = jnp.zeros((32, 128), F32)
    for ry, rx in hidden_peers:
        slot = POS[(-ry) % Y] * X + (-rx) % X
        links.push(
            leaving.at[pl.ds(pl.multiple_of(links.hidden(ry, rx) * 8, 8), 8)],
            landed.at[pl.ds(slot * 8, 8)],
            dict(ry=ry, rx=rx),
            ("landed", slot < 16),
        )
    landed[0:8] = leaving[pl.ds(pl.multiple_of(h * 8, 8), 8)]

    along_f32, along, whole, whole_f32 = s["along_f32"], s["along"], s["whole"], s["whole_f32"]
    feature_rows, product = s["feature_rows"], s["product"]

    def pass_along(half):
        p0, p1 = HALVES[half]
        span = slice(p0 * 12, p1 * 12)
        part = pl.ds(p0 * 12, 48)
        links.arrive(landed.at[pl.ds(p0 * 32, (16 if half else 15) * 8)], ("landed", half == 0))
        for step in range(2):
            for k in range(3):
                along_f32[step, pl.ds(p0 * 12 + k, 16, stride=3), :] = landed[
                    pl.ds(p0 * 32 + step * 4 + k, 16, stride=8), :
                ]
            along[step, span] = along_f32[step, span].astype(BF16)
        for rz, rc in width_peers:
            links.push(along.at[links.core(rc), part], whole.at[w, part], dict(rz=rz, rc=rc), ("whole", half))
        whole[w, span] = along[c, span]

    def multiply(half):
        p0, p1 = HALVES[half]
        span = slice(p0 * 12, p1 * 12)
        links.arrive(whole.at[pl.ds(0, 15), pl.ds(p0 * 12, 48)], ("whole", half))
        for row in range(16):
            whole_f32[row, span] = whole[row, span].astype(F32)
            for k in range(3):
                feature_rows[k, pl.ds(p0 * 64 + row, 16, stride=16), :] = whole_f32[
                    row, pl.ds(p0 * 12 + k, 16, stride=3), :
                ]
        operand = jnp.concatenate([feature_rows[k, p0 * 64 : p1 * 64] for k in range(3)], axis=1).astype(BF16)
        if half:
            links.arrive(out_w.at[1 - c], "out_w")
        for side in (0, 1):
            product[p0 * 64 : p1 * 64, side * WIDTH_DEV : (side + 1) * WIDTH_DEV] = jnp.dot(
                operand, out_w[side], preferred_element_type=F32
            )

    pass_along(1)
    pass_along(0)

    staged = {"a": s["sa"], "b": s["sb"]}
    landing = {"a": s["la"], "b": s["lb"]}
    columns = {"a": slice(0, CUT), "b": slice(CUT, WIDTH_CHIP)}
    multiplied = set()

    def summed(part, ry, rx):
        half = 1 if POS[ry] >= 4 else 0
        if half not in multiplied:
            multiplied.add(half)
            multiply(half)
        at = (POS[ry] * X + rx) * 16
        terms = [product[at : at + 16, columns[part]]]
        for _, _, key in reached(part, ry, rx):
            slot = landing[part].at[POS[key[1]], key[2]]
            links.arrive(slot, ("sum",) + key)
            terms.append(slot[...].astype(F32))
        return sum_all(terms)

    multiplied.add(1)
    multiply(1)
    for key in reversed(ARRIVAL_ORDER):
        part, ry, rx = key
        at = (POS[ry], rx)
        staged[part][at] = summed(*key).astype(BF16)
        dy, dx = BEFORE[key]
        links.push(staged[part].at[at], landing[part].at[at], dict(ry=dy, rx=dx), ("sum",) + key)
    done = jnp.concatenate([summed("a", 0, 0), summed("b", 0, 0)], axis=1).astype(BF16)
    result, swapped = s["result"], s["swapped"]
    for side in (0, 1):
        result[side] = done[:, side * WIDTH_DEV : (side + 1) * WIDTH_DEV]
    links.push(result.at[1 - c], swapped.at[c], dict(rc=1), "swapped")
    out[c] = result[c]
    links.arrive(swapped.at[1 - c], "swapped")
    out[1 - c] = swapped[1 - c]
    links.finish()
    assert len(links.keys) <= ARRIVALS


SCRATCH = dict(
    own_rows=((2, 16, WIDTH_DEV + 128), BF16),
    both=((2, 16, WIDTH_DEV + 128), BF16),
    weight_sums=((16, 8, 128), F32),
    joint=((WIDTH_CHIP, JOINT), BF16),
    keyval_w=((16, WIDTH_DEV), BF16),
    out_w=((2, FEAT_DEV, WIDTH_DEV), BF16),
    keys=((CACHE, HEAD_DIM), BF16),
    values=((CACHE, HEAD_DIM), BF16),
    ga=((Y, X, 16, CUT), BF16),
    gb=((Y, X, 16, REST + 128), BF16),
    acc=((4, 512, 128), F32),
    spread_out=((16, 128, 128), F32),
    packed=((16, 128, 128), BF16),
    shares=((16, 128, 128), BF16),
    each=((Z, 128, 128), F32),
    total=((128, 128), F32),
    owned=((256, 128), F32),
    queries=((256, 128), F32),
    blocks=((192, 128), F32),
    att_blocks=((192, 128), F32),
    leaving=((256, 128), F32),
    landed=((256, 128), F32),
    along_f32=((2, 96, 128), F32),
    along=((2, 96, 128), BF16),
    whole=((16, 96, 128), BF16),
    whole_f32=((16, 96, 128), F32),
    feature_rows=((3, 512, 128), F32),
    product=((512, WIDTH_CHIP), F32),
    sa=((Y, X, 16, CUT), BF16),
    sb=((Y, X, 16, REST), BF16),
    la=((Y, X, 16, CUT), BF16),
    lb=((Y, X, 16, REST), BF16),
    result=((2, 16, WIDTH_DEV), BF16),
    swapped=((2, 16, WIDTH_DEV), BF16),
)


def shards(tokens, gain, query_weight, keyval_weight, out_weight, key_cache, value_cache, lengths):
    names = list(SCRATCH)

    def body(*refs):
        scratch = dict(zip(names, refs[9:]))
        scratch.update(send_sem=refs[-3], recv_sems=refs[-2], local_sems=refs[-1])
        kernel(*refs[:9], scratch)

    vmem, smem, hbm = (pl.BlockSpec(memory_space=space) for space in (pltpu.VMEM, pltpu.SMEM, pl.ANY))
    return pl.pallas_call(
        body,
        out_shape=jax.ShapeDtypeStruct(tokens.shape, BF16),
        in_specs=[vmem, vmem, smem, hbm, hbm, hbm, hbm, hbm],
        out_specs=vmem,
        scratch_shapes=[pltpu.VMEM(shape, dtype) for shape, dtype in SCRATCH.values()]
        + [
            pltpu.SemaphoreType.DMA((1,)),
            pltpu.SemaphoreType.DMA((ARRIVALS,)),
            pltpu.SemaphoreType.DMA((5,)),
        ],
        compiler_params=pltpu.CompilerParams(
            collective_id=0, has_side_effects=True, vmem_limit_bytes=VMEM_BYTES
        ),
    )(tokens, gain, lengths, query_weight, keyval_weight.T, out_weight, key_cache, value_cache)


def solution(mesh):
    return jax.shard_map(
        shards,
        mesh=mesh,
        in_specs=(
            P(None, "hidden", "width"),
            P("width"),
            P("width", "hidden"),
            P("width", "hidden"),
            P("hidden", "width"),
            P(("hidden", "width"), None, None),
            P(("hidden", "width"), None, None),
            P(("hidden", "width")),
        ),
        out_specs=P(None, "hidden", "width"),
        check_vma=False,
    )
```

time: 114 us -> 96.8 us (0.85)
  Pallas kernels: 106 us -> 94.5 us
  local copies, waits for them, and re-layouts: 7.13 us -> 1.52 us
    pallas_call x1, Pallas kernels: 106 us -> 94.5 us  [shards(): pl.pallas_call(body, out_shape=jax.ShapeDtypeStruct(tokens.shape, BF16),...]
    unnamed x12 -> x1, local copies, waits for them, and re-layouts: 6.43 us -> 1.52 us
where the time goes in v2:
time: 96.8 us; the launch traced here: 96.6 us
  Pallas kernels  94.5 us (98%)
  local copies, waits for them, and re-layouts  1.52 us (2%)
    pallas_call x1, Pallas kernels, shards(): pl.pallas_call(body, out_shape=jax.ShapeDtypeStruct(tokens.shape, BF16),...  94.5 us

profile of v2, /device:TPU:1, one launch (start us, length us, event | category | flops | bytes accessed | tf_op | source)
XLA Modules:
  0.0 96.6 jit_solution(11825407654126287296)
XLA Ops:
  0.7 94.5 %shard_map.82 = bf16[2,16,1152]{2,1,0:T(8,128)(2,1)} custom-call(bf16[2,16,1152]{2,1,0:T(8,128)(2,1)} %refs_0_.1, f32[1152]{0:T(1024)} %refs_1_.1, s32[1]{0:T(128)S(6)} %copy.10.refs_2_, bf16[1152,384]{1,0:T(8,128)(2,1)} %refs_3_.1, bf16[16,1152]{1,0:T(8,128)(2,1)} %bitcast.1, bf16[384,1152]{1,0:T(8,128)(2,1)} %refs_5_.1, bf16[1,2048,256]{2,1,0:T(8,128)(2,1)} %refs_6_.1, ...), custom_call_target="tpu_custom_call" | custom-call | tf_op jit(solution)/shard_map/pallas_call | solution.py:510
  95.1 1.5 %copy.11 = bf16[2,16,1152]{2,1,0:T(8,128)(2,1)} copy(bf16[2,16,1152]{2,1,0:T(8,128)(2,1)} %shard_map.82) | data formatting | bytes 147456

commit v3 on v2

--- a/solution.py
+++ b/solution.py
@@ -20,28 +20,41 @@
 MASKED_SCORE = -1e30
 
 X, Y, Z = 4, 8, 8
-CUT = 1024
-REST = WIDTH_CHIP - CUT
+BLOCK = WIDTH_DEV + 128
 ORDER = (0, 1, 7, 2, 6, 3, 5, 4)
 POS = {ry: pos for pos, ry in enumerate(ORDER)}
 CHUNKS = ((0, 3), (3, 5), (5, 7), (7, 8))
-HALVES = ((0, 4), (4, 8))
+BACK = ((0, 3, 0, 48), (3, 5, 48, 32), (5, 7, 80, 32), (7, 8, 112, 16))
 STAT = 16
 
-VMEM_BYTES = 60 * 1024 * 1024
-ARRIVALS = 144
+VMEM_BYTES = 55100 * 1024
+ARRIVALS = 80
 ARRIVAL_ORDER = (
-    ("b", 7, 0), ("b", 1, 0), ("b", 0, 3), ("b", 0, 1), ("a", 0, 3), ("a", 0, 1),
-    ("b", 6, 0), ("b", 2, 0), ("a", 7, 0), ("a", 1, 0), ("a", 0, 2), ("b", 7, 3),
-    ("b", 7, 1), ("a", 7, 3), ("a", 1, 3), ("b", 1, 3), ("b", 1, 1), ("a", 7, 1),
-    ("a", 1, 1), ("b", 0, 2), ("b", 5, 0), ("b", 6, 1), ("b", 3, 0), ("b", 6, 3),
-    ("a", 6, 0), ("a", 2, 0), ("b", 2, 1), ("b", 2, 3), ("a", 7, 2), ("a", 1, 2),
-    ("a", 6, 3), ("a", 2, 3), ("b", 1, 2), ("b", 7, 2), ("a", 6, 1), ("a", 2, 1),
-    ("b", 4, 0), ("b", 5, 3), ("b", 5, 1), ("a", 3, 0), ("a", 5, 0), ("b", 3, 3),
-    ("b", 3, 1), ("a", 2, 2), ("a", 6, 2), ("a", 3, 3), ("b", 6, 2), ("b", 2, 2),
-    ("a", 5, 3), ("a", 3, 1), ("a", 5, 1), ("b", 4, 3), ("b", 4, 1), ("a", 4, 0),
-    ("a", 3, 2), ("b", 3, 2), ("a", 5, 2), ("a", 4, 3), ("a", 4, 1), ("b", 4, 2),
-    ("b", 5, 2), ("a", 4, 2),
+    ("a", 0, 3), ("a", 0, 1), ("b", 7, 0), ("b", 1, 0), ("b", 0, 3), ("a", 0, 2),
+    ("b", 6, 0), ("b", 2, 0), ("b", 0, 1), ("a", 7, 0), ("a", 1, 0), ("a", 7, 3),
+    ("a", 1, 3), ("b", 7, 3), ("b", 7, 1), ("a", 7, 1), ("a", 1, 1), ("b", 1, 3),
+    ("b", 1, 1), ("b", 0, 2), ("a", 7, 2), ("a", 1, 2), ("b", 6, 1), ("b", 6, 3),
+    ("b", 5, 0), ("b", 3, 0), ("b", 2, 1), ("b", 2, 3), ("a", 6, 0), ("a", 2, 0),
+    ("b", 7, 2), ("b", 1, 2), ("a", 6, 3), ("a", 2, 3), ("a", 6, 1), ("a", 2, 1),
+    ("b", 6, 2), ("a", 6, 2), ("a", 2, 2), ("b", 5, 1), ("b", 5, 3), ("b", 4, 0),
+    ("a", 3, 0), ("b", 3, 1), ("b", 3, 3), ("a", 5, 0), ("a", 3, 3), ("b", 2, 2),
+    ("a", 5, 3), ("a", 3, 1), ("a", 5, 1), ("a", 3, 2), ("b", 5, 2), ("a", 5, 2),
+    ("b", 4, 1), ("b", 4, 3), ("a", 4, 0), ("a", 4, 3), ("b", 4, 2), ("b", 3, 2),
+    ("a", 4, 1), ("a", 4, 2),
+)
+
+RETURN_ORDER = (
+    ("a", 4, 2), ("a", 4, 1), ("a", 4, 3), ("b", 4, 2), ("b", 4, 1), ("b", 4, 3),
+    ("a", 4, 0), ("a", 5, 2), ("b", 3, 2), ("b", 5, 2), ("a", 3, 1), ("a", 5, 3),
+    ("b", 3, 3), ("b", 5, 1), ("a", 3, 0), ("a", 3, 2), ("a", 5, 1), ("a", 3, 3),
+    ("a", 5, 0), ("b", 4, 0), ("b", 2, 2), ("b", 6, 2), ("b", 2, 3), ("b", 6, 1),
+    ("a", 6, 2), ("b", 3, 1), ("b", 5, 3), ("a", 2, 1), ("a", 6, 3), ("a", 2, 0),
+    ("a", 6, 1), ("a", 2, 2), ("b", 1, 2), ("b", 7, 2), ("b", 0, 2), ("b", 1, 3),
+    ("b", 7, 1), ("b", 0, 1), ("a", 6, 0), ("b", 2, 1), ("b", 6, 3), ("a", 2, 3),
+    ("a", 1, 1), ("a", 7, 2), ("b", 3, 0), ("b", 5, 0), ("a", 1, 0), ("a", 7, 3),
+    ("a", 1, 2), ("a", 7, 1), ("b", 1, 1), ("b", 7, 3), ("a", 7, 0), ("a", 1, 3),
+    ("b", 0, 3), ("b", 2, 0), ("b", 6, 0), ("b", 1, 0), ("b", 7, 0), ("a", 0, 2),
+    ("a", 0, 1), ("a", 0, 3),
 )
 
 
@@ -52,7 +65,7 @@
             along = [(1, 0)]
         if ry in (1, 2) or (ry == 3 and rx >= 2):
             along = [(-1, 0)]
-        return along + ([(0, 1), (0, -1), (0, 2)] if (ry, rx) == (0, 0) else [])
+        return ([(0, 1), (0, -1), (0, 2)] if (ry, rx) == (0, 0) else []) + along
     if rx == 0:
         along = {0: [(1, 0), (-1, 0), (2, 0), (-2, 0)], 6: [(1, 0)], 5: [(1, 0)], 2: [(-1, 0)]}.get(ry, [])
         return along + [(0, 1), (0, -1)] + ([(0, 2)] if ry == 4 else [])
@@ -72,6 +85,8 @@
     for rx in range(X)
     for dy, dx, key in reached(part, ry, rx)
 }
+
+CROSSED = ((0, 1), (0, 3), (0, 2), (1, 0), (7, 0), (2, 0), (6, 0))
 
 
 class Links:
@@ -95,17 +110,18 @@
     def core(self, rc):
         return self.c if rc == 0 else 1 - self.c
 
-    def device(self, ry=0, rx=0, rz=0, rc=0):
-        at = (ry % Y, rx % X, rz % Z, rc)
+    def device(self, ry=0, rx=0, rz=0, rc=0, core=None):
+        at = (ry % Y, rx % X, rz % Z, rc, core)
         if at not in self.devices:
-            self.devices[at] = {"hidden": self.hidden(*at[:2]), "width": self.width(*at[2:])}
+            width = self.width(*at[2:4]) if core is None else self.z * 2 + core
+            self.devices[at] = {"hidden": self.hidden(*at[:2]), "width": width}
         return self.devices[at]
 
     def arrival(self, key):
         return self.recv_sems.at[self.keys.setdefault(key, len(self.keys))]
 
-    def push(self, src, dst, to, key):
-        copy = pltpu.make_async_remote_copy(
+    def copy(self, src, dst, to, key):
+        return pltpu.make_async_remote_copy(
             src_ref=src,
             dst_ref=dst,
             send_sem=self.send_sem.at[0],
@@ -113,6 +129,9 @@
             device_id=self.device(**to),
             device_id_type=MESH,
         )
+
+    def push(self, src, dst, to, key):
+        copy = self.copy(src, dst, to, key)
         copy.start()
         self.sent.append(copy)
 
@@ -155,16 +174,25 @@
     width_peers = [(rz, rc) for rz in (4, 3, 5, 2, 6, 1, 7, 0) for rc in (0, 1) if (rz, rc) != (0, 0)]
     hidden_peers = [(ry, rx) for ry in reversed(ORDER) for rx in (2, 1, 3, 0) if (ry, rx) != (0, 0)]
 
+    local = s["local_sems"]
+    first_loads = [
+        pltpu.make_async_copy(tokens, s["tokens"], local.at[5]),
+        pltpu.make_async_copy(gain, s["gain"], local.at[6]),
+    ]
+    for load in first_loads:
+        load.start()
+
     barrier = pltpu.get_barrier_semaphore()
     for rz, rc in width_peers:
         pl.semaphore_signal(barrier, inc=1, device_id=links.device(rz=rz, rc=rc), device_id_type=MESH)
     for ry, rx in hidden_peers:
         pl.semaphore_signal(barrier, inc=1, device_id=links.device(ry=ry, rx=rx), device_id_type=MESH)
+    for ry, rx in CROSSED:
+        pl.semaphore_signal(barrier, inc=1, device_id=links.device(ry=ry, rx=rx, rc=1), device_id_type=MESH)
 
     joint, out_w = s["joint"], s["out_w"]
     mine = pl.ds(pl.multiple_of(c * WIDTH_DEV, WIDTH_DEV), WIDTH_DEV)
     others = pl.ds(pl.multiple_of((1 - c) * WIDTH_DEV, WIDTH_DEV), WIDTH_DEV)
-    local = s["local_sems"]
     loads = [
         pltpu.make_async_copy(keyval_weight, s["keyval_w"], local.at[0]),
         pltpu.make_async_copy(query_weight, joint.at[mine, pl.ds(0, FEAT_DEV)], local.at[1]),
@@ -175,8 +203,10 @@
     for load in loads:
         load.start()
 
-    gain_row = gain[...][None]
-    rows = tokens[...].astype(F32).reshape(32, WIDTH_DEV)
+    for load in first_loads:
+        load.wait()
+    gain_row = s["gain"][...][None]
+    rows = s["tokens"][...].astype(F32).reshape(32, WIDTH_DEV)
     own_mean = jnp.sum(rows, axis=1, keepdims=True) * (1.0 / WIDTH_DEV)
     centered = rows - own_mean
     own_spread = jnp.sum(centered * centered, axis=1, keepdims=True)
@@ -184,29 +214,44 @@
     lanes = jnp.zeros((32, 128), F32)
     for at, piece in enumerate(pieces(own_mean) + pieces(own_spread)):
         lanes = jnp.where(lane == at, piece.astype(F32), lanes)
-    own_rows, both = s["own_rows"], s["both"]
-    own_rows[...] = jnp.concatenate([centered * gain_row, lanes], axis=1).astype(BF16).reshape(2, 16, WIDTH_DEV + 128)
-    both[c] = own_rows[c]
-
-    pl.semaphore_wait(barrier, len(width_peers) + len(hidden_peers))
-    links.push(own_rows.at[1 - c], both.at[c], dict(rc=1), "both")
-
-    ga, gb = s["ga"], s["gb"]
-    block = {"a": ga, "b": gb}
+    own_rows = s["own_rows"]
+    own_rows[...] = jnp.concatenate([centered * gain_row, lanes], axis=1).astype(BF16).reshape(2, 16, BLOCK)
+
+    block = {"a": s["ga"], "b": s["gb"]}
+    parts = "ab"
+
+    def first_copies(side):
+        part = parts[side]
+        to_other = [(0, 0, (part, 0, 0))]
+        for step in (side, 1 - side):
+            for dy, dx, key in reached(part, 0, 0) + (to_other if step != side else []):
+                yield links.copy(
+                    own_rows.at[step],
+                    block[part].at[POS[key[1]], key[2]],
+                    dict(ry=dy, rx=dx, core=step),
+                    key if (dy, dx) != (0, 0) else "own chip",
+                )
+
+    for part in parts:
+        for dy, dx, _ in reached(part, 0, 0) + [(0, 0, None)]:
+            for step in (0, 1):
+                links.device(ry=dy, rx=dx, core=step)
+
+    pl.semaphore_wait(barrier, len(width_peers) + len(hidden_peers) + len(CROSSED))
+
+    for side in (0, 1):
+
+        @pl.when(c == side)
+        def _(side=side):
+            for copy in first_copies(side):
+                copy.start()
+            block[parts[side]][0, 0] = own_rows[side]
 
     def pass_on(part, ry, rx):
         for dy, dx, key in reached(part, ry, rx):
             links.push(
                 block[part].at[POS[ry], rx], block[part].at[POS[key[1]], key[2]], dict(ry=dy, rx=dx), key
             )
-
-    links.arrive(both.at[1 - c], "both")
-    ga[0, 0] = both[0, :, :CUT]
-    gb[0, 0] = jnp.concatenate(
-        [both[0, :, CUT:WIDTH_DEV], both[1, :, :WIDTH_DEV], both[0, :, WIDTH_DEV:] + both[1, :, WIDTH_DEV:]], axis=1
-    )
-    pass_on("b", 0, 0)
-    pass_on("a", 0, 0)
 
     loads[0].wait()
     across = jnp.concatenate([s["keyval_w"][...].astype(F32), jnp.zeros((112, WIDTH_DEV), F32)], axis=0)
@@ -239,13 +284,23 @@
         count = p1 - p0
         if chunk == 0:
             links.arrive(joint.at[others], "joint")
-        stretch = gb[p0:p1].reshape(count * 64, REST + 128)
-        partial = jnp.dot(
-            ga[p0:p1].reshape(count * 64, CUT), joint[0:CUT], preferred_element_type=F32
-        ) + jnp.dot(stretch[:, :REST], joint[CUT:WIDTH_CHIP], preferred_element_type=F32)
-        for k in range(4):
-            columns = partial[:, k * 128 : (k + 1) * 128]
-            acc[k, p0 * 64 : p1 * 64] = columns if k < 3 else columns + stretch[:, REST:].astype(F32)
+            links.arrive(block["a"].at[0, 0], "own chip")
+        sides = [block[part][p0:p1].reshape(count * 64, BLOCK) for part in parts]
+        partial = sum_all(
+            [
+                jnp.dot(
+                    rows_of[:, :WIDTH_DEV],
+                    joint[side * WIDTH_DEV : (side + 1) * WIDTH_DEV],
+                    preferred_element_type=F32,
+                )
+                for side, rows_of in enumerate(sides)
+            ]
+        )
+        for k in range(3):
+            acc[k, p0 * 64 : p1 * 64] = partial[:, k * 128 : (k + 1) * 128]
+        acc[3, p0 * 64 : p1 * 64] = partial[:, FEAT_DEV:JOINT] + sum_all(
+            [rows_of[:, WIDTH_DEV:].astype(F32) for rows_of in sides]
+        )
         span = slice(p0 * 16, p1 * 16)
         for row in range(16):
             for k in range(4):
@@ -308,7 +363,6 @@
                     links.push(owned.at[tile], queries.at[here_h], dict(ry=ry, rx=rx), "queries")
 
     missing = [{key for key in ARRIVAL_ORDER if p0 <= POS[key[1]] < p1} for p0, p1 in CHUNKS]
-    waiting = []
     for key in ARRIVAL_ORDER:
         part, ry, rx = key
         links.arrive(block[part].at[POS[ry], rx], key)
@@ -318,10 +372,7 @@
                 missing[chunk].discard(key)
                 if not missing[chunk]:
                     project(chunk)
-                    if waiting:
-                        hand_out(waiting.pop(0))
-                    waiting.append(chunk)
-    for chunk in waiting:
+    for chunk in range(len(CHUNKS)):
         hand_out(chunk)
 
     links.arrive(queries.at[pl.ds(0, 31 * 8)], "queries")
@@ -373,104 +424,127 @@
         for k in range(3):
             leaving[pl.ds(step * 4 + k, 32, stride=8), :] = att_blocks[pl.ds(step * 96 + k, 32, stride=3), :]
         leaving[pl.ds(step * 4 + 3, 32, stride=8), :] = jnp.zeros((32, 128), F32)
+
+    def back_part(pos):
+        return [part for part, (p0, p1, _, _) in enumerate(BACK) if p0 <= pos < p1][0]
+
     for ry, rx in hidden_peers:
         slot = POS[(-ry) % Y] * X + (-rx) % X
         links.push(
             leaving.at[pl.ds(pl.multiple_of(links.hidden(ry, rx) * 8, 8), 8)],
             landed.at[pl.ds(slot * 8, 8)],
             dict(ry=ry, rx=rx),
-            ("landed", slot < 16),
+            ("landed", back_part(slot // X)),
         )
     landed[0:8] = leaving[pl.ds(pl.multiple_of(h * 8, 8), 8)]
 
     along_f32, along, whole, whole_f32 = s["along_f32"], s["along"], s["whole"], s["whole_f32"]
     feature_rows, product = s["feature_rows"], s["product"]
 
-    def pass_along(half):
-        p0, p1 = HALVES[half]
-        span = slice(p0 * 12, p1 * 12)
-        part = pl.ds(p0 * 12, 48)
-        links.arrive(landed.at[pl.ds(p0 * 32, (16 if half else 15) * 8)], ("landed", half == 0))
+    def pass_along(part):
+        p0, p1, first, held = BACK[part]
+        count = (p1 - p0) * X
+        span = slice(first, first + held)
+        links.arrive(landed.at[pl.ds(p0 * 32, (count if p0 else count - 1) * 8)], ("landed", part))
         for step in range(2):
             for k in range(3):
-                along_f32[step, pl.ds(p0 * 12 + k, 16, stride=3), :] = landed[
-                    pl.ds(p0 * 32 + step * 4 + k, 16, stride=8), :
+                along_f32[step, pl.ds(first + k, count, stride=3), :] = landed[
+                    pl.ds(p0 * 32 + step * 4 + k, count, stride=8), :
                 ]
+            if count * 3 < held:
+                along_f32[step, first + count * 3 : first + held] = jnp.zeros((held - count * 3, 128), F32)
             along[step, span] = along_f32[step, span].astype(BF16)
         for rz, rc in width_peers:
-            links.push(along.at[links.core(rc), part], whole.at[w, part], dict(rz=rz, rc=rc), ("whole", half))
+            links.push(
+                along.at[links.core(rc), pl.ds(first, held)],
+                whole.at[w, pl.ds(first, held)],
+                dict(rz=rz, rc=rc),
+                ("whole", part),
+            )
         whole[w, span] = along[c, span]
 
-    def multiply(half):
-        p0, p1 = HALVES[half]
-        span = slice(p0 * 12, p1 * 12)
-        links.arrive(whole.at[pl.ds(0, 15), pl.ds(p0 * 12, 48)], ("whole", half))
+    def multiply(part):
+        p0, p1, first, held = BACK[part]
+        count = (p1 - p0) * X
+        span = slice(first, first + held)
+        links.arrive(whole.at[pl.ds(0, 15), pl.ds(first, held)], ("whole", part))
         for row in range(16):
             whole_f32[row, span] = whole[row, span].astype(F32)
             for k in range(3):
-                feature_rows[k, pl.ds(p0 * 64 + row, 16, stride=16), :] = whole_f32[
-                    row, pl.ds(p0 * 12 + k, 16, stride=3), :
+                feature_rows[k, pl.ds(p0 * 64 + row, count, stride=16), :] = whole_f32[
+                    row, pl.ds(first + k, count, stride=3), :
                 ]
         operand = jnp.concatenate([feature_rows[k, p0 * 64 : p1 * 64] for k in range(3)], axis=1).astype(BF16)
-        if half:
-            links.arrive(out_w.at[1 - c], "out_w")
         for side in (0, 1):
-            product[p0 * 64 : p1 * 64, side * WIDTH_DEV : (side + 1) * WIDTH_DEV] = jnp.dot(
-                operand, out_w[side], preferred_element_type=F32
-            )
-
-    pass_along(1)
-    pass_along(0)
+            product[side, p0 * 64 : p1 * 64] = jnp.dot(operand, out_w[side], preferred_element_type=F32)
+
+    for part in (3, 2, 1, 0):
+        pass_along(part)
+    links.arrive(out_w.at[1 - c], "out_w")
 
     staged = {"a": s["sa"], "b": s["sb"]}
     landing = {"a": s["la"], "b": s["lb"]}
-    columns = {"a": slice(0, CUT), "b": slice(CUT, WIDTH_CHIP)}
+    last, crossing = s["last"], s["crossing"]
     multiplied = set()
 
     def summed(part, ry, rx):
-        half = 1 if POS[ry] >= 4 else 0
-        if half not in multiplied:
-            multiplied.add(half)
-            multiply(half)
+        back = back_part(POS[ry])
+        if back not in multiplied:
+            multiplied.add(back)
+            multiply(back)
         at = (POS[ry] * X + rx) * 16
-        terms = [product[at : at + 16, columns[part]]]
+        terms = [product[parts.index(part), at : at + 16]]
         for _, _, key in reached(part, ry, rx):
             slot = landing[part].at[POS[key[1]], key[2]]
-            links.arrive(slot, ("sum",) + key)
+            links.arrive(slot, key)
             terms.append(slot[...].astype(F32))
         return sum_all(terms)
 
-    multiplied.add(1)
-    multiply(1)
-    for key in reversed(ARRIVAL_ORDER):
+    for key in RETURN_ORDER:
         part, ry, rx = key
         at = (POS[ry], rx)
         staged[part][at] = summed(*key).astype(BF16)
         dy, dx = BEFORE[key]
-        links.push(staged[part].at[at], landing[part].at[at], dict(ry=dy, rx=dx), ("sum",) + key)
-    done = jnp.concatenate([summed("a", 0, 0), summed("b", 0, 0)], axis=1).astype(BF16)
-    result, swapped = s["result"], s["swapped"]
+        first_keys = [first_key for _, _, first_key in reached(part, 0, 0)]
+        if key in first_keys:
+            slot = 1 + 2 * first_keys.index(key) + c
+            links.push(
+                staged[part].at[at], last.at[slot], dict(ry=dy, rx=dx, core=parts.index(part)), "last"
+            )
+        else:
+            links.push(staged[part].at[at], landing[part].at[at], dict(ry=dy, rx=dx), key)
+    crossing[...] = product[1 - c, 0:16].astype(BF16)
+    links.push(crossing, last.at[0], dict(rc=1), "last")
+
     for side in (0, 1):
-        result[side] = done[:, side * WIDTH_DEV : (side + 1) * WIDTH_DEV]
-    links.push(result.at[1 - c], swapped.at[c], dict(rc=1), "swapped")
-    out[c] = result[c]
-    links.arrive(swapped.at[1 - c], "swapped")
-    out[1 - c] = swapped[1 - c]
+
+        @pl.when(c == side)
+        def _(side=side):
+            count = len(reached(parts[side], 0, 0))
+            links.arrive(last.at[pl.ds(0, 1 + 2 * count)], "last")
+            for step in range(2):
+                terms = [product[side, 0:16]] if step == side else [last[0].astype(F32)]
+                terms += [last[1 + 2 * at + step].astype(F32) for at in range(count)]
+                out[step] = sum_all(terms).astype(BF16)
+            for copy in first_copies(side):
+                copy.wait_send()
+
     links.finish()
     assert len(links.keys) <= ARRIVALS
 
 
 SCRATCH = dict(
-    own_rows=((2, 16, WIDTH_DEV + 128), BF16),
-    both=((2, 16, WIDTH_DEV + 128), BF16),
+    tokens=((2, 16, WIDTH_DEV), BF16),
+    gain=((WIDTH_DEV,), F32),
+    own_rows=((2, 16, BLOCK), BF16),
     weight_sums=((16, 8, 128), F32),
     joint=((WIDTH_CHIP, JOINT), BF16),
     keyval_w=((16, WIDTH_DEV), BF16),
     out_w=((2, FEAT_DEV, WIDTH_DEV), BF16),
     keys=((CACHE, HEAD_DIM), BF16),
     values=((CACHE, HEAD_DIM), BF16),
-    ga=((Y, X, 16, CUT), BF16),
-    gb=((Y, X, 16, REST + 128), BF16),
+    ga=((Y, X, 16, BLOCK), BF16),
+    gb=((Y, X, 16, BLOCK), BF16),
     acc=((4, 512, 128), F32),
     spread_out=((16, 128, 128), F32),
     packed=((16, 128, 128), BF16),
@@ -483,18 +557,18 @@
     att_blocks=((192, 128), F32),
     leaving=((256, 128), F32),
     landed=((256, 128), F32),
-    along_f32=((2, 96, 128), F32),
-    along=((2, 96, 128), BF16),
-    whole=((16, 96, 128), BF16),
-    whole_f32=((16, 96, 128), F32),
+    along_f32=((2, 128, 128), F32),
+    along=((2, 128, 128), BF16),
+    whole=((16, 128, 128), BF16),
+    whole_f32=((16, 128, 128), F32),
     feature_rows=((3, 512, 128), F32),
-    product=((512, WIDTH_CHIP), F32),
-    sa=((Y, X, 16, CUT), BF16),
-    sb=((Y, X, 16, REST), BF16),
-    la=((Y, X, 16, CUT), BF16),
-    lb=((Y, X, 16, REST), BF16),
-    result=((2, 16, WIDTH_DEV), BF16),
-    swapped=((2, 16, WIDTH_DEV), BF16),
+    product=((2, 512, WIDTH_DEV), F32),
+    sa=((Y, X, 16, WIDTH_DEV), BF16),
+    sb=((Y, X, 16, WIDTH_DEV), BF16),
+    la=((Y, X, 16, WIDTH_DEV), BF16),
+    lb=((Y, X, 16, WIDTH_DEV), BF16),
+    last=((13, 16, WIDTH_DEV), BF16),
+    crossing=((16, WIDTH_DEV), BF16),
 )
 
 
@@ -510,13 +584,13 @@
     return pl.pallas_call(
         body,
         out_shape=jax.ShapeDtypeStruct(tokens.shape, BF16),
-        in_specs=[vmem, vmem, smem, hbm, hbm, hbm, hbm, hbm],
+        in_specs=[hbm, hbm, smem, hbm, hbm, hbm, hbm, hbm],
         out_specs=vmem,
         scratch_shapes=[pltpu.VMEM(shape, dtype) for shape, dtype in SCRATCH.values()]
         + [
             pltpu.SemaphoreType.DMA((1,)),
             pltpu.SemaphoreType.DMA((ARRIVALS,)),
-            pltpu.SemaphoreType.DMA((5,)),
+            pltpu.SemaphoreType.DMA((7,)),
         ],
         compiler_params=pltpu.CompilerParams(
             collective_id=0, has_side_effects=True, vmem_limit_bytes=VMEM_BYTES

time: 96.8 us -> 85.8 us (0.89)
  Pallas kernels: 94.5 us -> 82.8 us
    pallas_call x1, Pallas kernels: 94.5 us -> 82.8 us  [shards(): pl.pallas_call(body, out_shape=jax.ShapeDtypeStruct(tokens.shape, BF16),...]
    unnamed x1 -> x5, local copies, waits for them, and re-layouts: 1.52 us -> 2.09 us
where the time goes in v3:
time: 85.8 us; the launch traced here: 85.5 us
  Pallas kernels  82.8 us (97%)
  local copies, waits for them, and re-layouts  2.09 us (2%)
    pallas_call x1, Pallas kernels, shards(): pl.pallas_call(body, out_shape=jax.ShapeDtypeStruct(tokens.shape, BF16),...  82.8 us
    unnamed x5, local copies, waits for them, and re-layouts  2.09 us

profile of v3, /device:TPU:1, one launch (start us, length us, event | category | flops | bytes accessed | tf_op | source)
XLA Modules:
  0.0 85.5 jit_solution(15557938228833110223)
XLA Ops:
  0.7 0.0 copy-start
  0.7 0.8 copy-done
  1.4 0.0 copy-start.1
  1.4 0.7 copy-done.1
  2.1 82.8 %shard_map.82 = bf16[2,16,1152]{2,1,0:T(8,128)(2,1)S(1)} custom-call(bf16[2,16,1152]{2,1,0:T(8,128)(2,1)} %refs_0_.1, f32[1152]{0:T(1024)S(1)} %copy-done.1, s32[1]{0:T(128)S(6)} %copy.10.refs_2_, bf16[1152,384]{1,0:T(8,128)(2,1)} %refs_3_.1, bf16[16,1152]{1,0:T(8,128)(2,1)S(1)} %bitcast.1, bf16[384,1152]{1,0:T(8,128)(2,1)} %refs_5_.1, ...), custom_call_target="tpu_custom_call" | custom-call | tf_op jit(solution)/shard_map/pallas_call | solution.py:584
  84.9 0.6 copy.11
Async XLA Ops:
  0.7 0.8 copy-start
  1.4 0.7 copy-start.1

commit v4 on v3

--- a/solution.py
+++ b/solution.py
@@ -23,12 +23,12 @@
 BLOCK = WIDTH_DEV + 128
 ORDER = (0, 1, 7, 2, 6, 3, 5, 4)
 POS = {ry: pos for pos, ry in enumerate(ORDER)}
-CHUNKS = ((0, 3), (3, 5), (5, 7), (7, 8))
-BACK = ((0, 3, 0, 48), (3, 5, 48, 32), (5, 7, 80, 32), (7, 8, 112, 16))
+CHUNKS = ((0, 1), (1, 3), (3, 5), (5, 7), (7, 8))
+BACK = ((0, 1, 0, 16), (1, 3, 16, 32), (3, 5, 48, 32), (5, 7, 80, 32), (7, 8, 112, 16))
 STAT = 16
 
 VMEM_BYTES = 55100 * 1024
-ARRIVALS = 80
+ARRIVALS = 84
 ARRIVAL_ORDER = (
     ("a", 0, 3), ("a", 0, 1), ("b", 7, 0), ("b", 1, 0), ("b", 0, 3), ("a", 0, 2),
     ("b", 6, 0), ("b", 2, 0), ("b", 0, 1), ("a", 7, 0), ("a", 1, 0), ("a", 7, 3),
@@ -49,10 +49,10 @@
     ("b", 3, 3), ("b", 5, 1), ("a", 3, 0), ("a", 3, 2), ("a", 5, 1), ("a", 3, 3),
     ("a", 5, 0), ("b", 4, 0), ("b", 2, 2), ("b", 6, 2), ("b", 2, 3), ("b", 6, 1),
     ("a", 6, 2), ("b", 3, 1), ("b", 5, 3), ("a", 2, 1), ("a", 6, 3), ("a", 2, 0),
-    ("a", 6, 1), ("a", 2, 2), ("b", 1, 2), ("b", 7, 2), ("b", 0, 2), ("b", 1, 3),
-    ("b", 7, 1), ("b", 0, 1), ("a", 6, 0), ("b", 2, 1), ("b", 6, 3), ("a", 2, 3),
+    ("b", 1, 2), ("b", 7, 2), ("b", 1, 3), ("b", 7, 1), ("a", 6, 1), ("a", 2, 2),
+    ("b", 0, 2), ("b", 0, 1), ("a", 6, 0), ("b", 2, 1), ("b", 6, 3), ("a", 2, 3),
     ("a", 1, 1), ("a", 7, 2), ("b", 3, 0), ("b", 5, 0), ("a", 1, 0), ("a", 7, 3),
-    ("a", 1, 2), ("a", 7, 1), ("b", 1, 1), ("b", 7, 3), ("a", 7, 0), ("a", 1, 3),
+    ("b", 1, 1), ("b", 7, 3), ("a", 1, 2), ("a", 7, 1), ("a", 1, 3), ("a", 7, 0),
     ("b", 0, 3), ("b", 2, 0), ("b", 6, 0), ("b", 1, 0), ("b", 7, 0), ("a", 0, 2),
     ("a", 0, 1), ("a", 0, 3),
 )
@@ -86,7 +86,7 @@
     for dy, dx, key in reached(part, ry, rx)
 }
 
-CROSSED = ((0, 1), (0, 3), (0, 2), (1, 0), (7, 0), (2, 0), (6, 0))
+NEAR = ((0, 1), (0, 3), (0, 2), (1, 0), (7, 0), (2, 0), (6, 0))
 
 
 class Links:
@@ -185,10 +185,10 @@
     barrier = pltpu.get_barrier_semaphore()
     for rz, rc in width_peers:
         pl.semaphore_signal(barrier, inc=1, device_id=links.device(rz=rz, rc=rc), device_id_type=MESH)
-    for ry, rx in hidden_peers:
-        pl.semaphore_signal(barrier, inc=1, device_id=links.device(ry=ry, rx=rx), device_id_type=MESH)
-    for ry, rx in CROSSED:
-        pl.semaphore_signal(barrier, inc=1, device_id=links.device(ry=ry, rx=rx, rc=1), device_id_type=MESH)
+    for ry, rx in NEAR:
+        for rc in (0, 1):
+            to = links.device(ry=ry, rx=rx, rc=rc)
+            pl.semaphore_signal(barrier, inc=1, device_id=to, device_id_type=MESH)
 
     joint, out_w = s["joint"], s["out_w"]
     mine = pl.ds(pl.multiple_of(c * WIDTH_DEV, WIDTH_DEV), WIDTH_DEV)
@@ -237,7 +237,7 @@
             for step in (0, 1):
                 links.device(ry=dy, rx=dx, core=step)
 
-    pl.semaphore_wait(barrier, len(width_peers) + len(hidden_peers) + len(CROSSED))
+    pl.semaphore_wait(barrier, len(width_peers) + 2 * len(NEAR))
 
     for side in (0, 1):
 
@@ -478,7 +478,7 @@
         for side in (0, 1):
             product[side, p0 * 64 : p1 * 64] = jnp.dot(operand, out_w[side], preferred_element_type=F32)
 
-    for part in (3, 2, 1, 0):
+    for part in (4, 3, 2, 1, 0):
         pass_along(part)
     links.arrive(out_w.at[1 - c], "out_w")
 
@@ -580,7 +580,7 @@
         scratch.update(send_sem=refs[-3], recv_sems=refs[-2], local_sems=refs[-1])
         kernel(*refs[:9], scratch)
 
-    vmem, smem, hbm = (pl.BlockSpec(memory_space=space) for space in (pltpu.VMEM, pltpu.SMEM, pl.ANY))
+    vmem, smem, hbm = (pl.BlockSpec(memory_space=space) for space in (pltpu.VMEM, pltpu.SMEM, pltpu.HBM))
     return pl.pallas_call(
         body,
         out_shape=jax.ShapeDtypeStruct(tokens.shape, BF16),

time: 85.8 us -> 84.1 us (0.980)
  Pallas kernels: 82.8 us -> 81.1 us
    pallas_call x1, Pallas kernels: 82.8 us -> 81.1 us  [shards(): pl.pallas_call(body, out_shape=jax.ShapeDtypeStruct(tokens.shape, BF16),...]
where the time goes in v4:
time: 84.1 us; the launch traced here: 83.9 us
  Pallas kernels  81.1 us (96%)
  local copies, waits for them, and re-layouts  2.09 us (2%)
    pallas_call x1, Pallas kernels, shards(): pl.pallas_call(body, out_shape=jax.ShapeDtypeStruct(tokens.shape, BF16),...  81.1 us
    unnamed x5, local copies, waits for them, and re-layouts  2.09 us

profile of v4, /device:TPU:1, one launch (start us, length us, event | category | flops | bytes accessed | tf_op | source)
XLA Modules:
  0.0 83.9 jit_solution(3243568231917109797)
XLA Ops:
  0.7 0.0 copy-start
  0.7 0.8 copy-done
  1.4 0.0 copy-start.1
  1.4 0.7 copy-done.1
  2.1 81.1 %shard_map.82 = bf16[2,16,1152]{2,1,0:T(8,128)(2,1)S(1)} custom-call(bf16[2,16,1152]{2,1,0:T(8,128)(2,1)} %refs_0_.1, f32[1152]{0:T(1024)S(1)} %copy-done.1, s32[1]{0:T(128)S(6)} %copy.10.refs_2_, bf16[1152,384]{1,0:T(8,128)(2,1)} %refs_3_.1, bf16[16,1152]{1,0:T(8,128)(2,1)S(1)} %bitcast.1, bf16[384,1152]{1,0:T(8,128)(2,1)} %refs_5_.1, ...), custom_call_target="tpu_custom_call" | custom-call | tf_op jit(solution)/shard_map/pallas_call | solution.py:584
  83.2 0.6 copy.11
Async XLA Ops:
  0.7 0.8 copy-start
  1.4 0.7 copy-start.1
